TPU v7x, 256 devices: a whole 4x4x8 slice. The times are simulated.
256 devices in a mesh: lon: 16 (over y_hi, x, core), lat: 16 (over z, y_lo).
Axes of the slice: x: 4, y: 4 (y_hi: 2, y_lo: 2; y = y_hi * 2 + y_lo), z: 8, core: 2. Of those that a mesh axis runs over, the one named last changes fastest.
Arguments:
- features: bfloat16 [48, 2, 128, 8192], P(None, None, 'lat', 'lon'), may hold values from -6 to 6
- spline_coef: bfloat16 [432, 480], replicated, may hold values from -0.25 to 0.25
- edge_mask: int32 [48, 48], replicated, may hold values 0 or 1
- head_weight: bfloat16 [2, 48], replicated, may hold values from -0.875 to 0.875
- land_mask: int32 [128, 8192], P('lat', 'lon'), may hold values 0 or 1
- shift_coef: float32 [128, 8192], P('lat', 'lon'), may hold values from 0.02 to 2
Outputs:
- tendency: bfloat16 [2, 2, 128, 8192], P(None, None, 'lat', 'lon')
- surface: float32 [128, 8192], P('lat', 'lon')
- residual: float32 [128, 8192], P('lat', 'lon')
Inputs may be any that keep to these rules, and one draw needn't show every extreme that they name: `edge_mask`: 1 keeps an edge. `land_mask`: 1 marks ocean.
All inputs are finite; a program needn't handle non-finite values. No bound on the sum of `land_mask` on one device may be relied on, other than what follows from the above.
Results may differ from a plain program's by a relative error of at most 0.014.
Values may be sent and summed in bfloat16 or wider, within the bound.
A program may use at most 128 MiB of HBM per device.

v0:
```python
import jax
import jax.numpy as jnp
from jax import lax
from jax.sharding import PartitionSpec as P

C = 48
NB = 9
L = 2
ITERS = 2


def extended(block, sides, width):
    for axis, dim in sides:
        count = lax.axis_size(axis)
        forward = [(i, i + 1) for i in range(count - 1)]
        forward.append((count - 1, 0))
        backward = [(target, source) for source, target in forward]
        low = lax.ppermute(
            lax.slice_in_dim(block, block.shape[dim] - width, None, axis=dim), axis, forward
        )
        high = lax.ppermute(lax.slice_in_dim(block, 0, width, axis=dim), axis, backward)
        block = jnp.concatenate([low, block, high], axis=dim)
    return block


def passed_along(value, axis, steps):
    count = lax.axis_size(axis)
    pairs = [(source, (source + steps) % count) for source in range(count)]
    return lax.ppermute(value, axis, pairs)


def passed_along_2(value, axis, steps):
    count = lax.axis_size(axis)
    leading, last = (max(0, -steps), min(count, count - steps))
    return lax.ppermute(value, axis, [(source, source + steps) for source in range(leading, last)])


def masked_weight(spline_coef, edge_mask):
    wide_mask = jnp.tile(jnp.repeat(edge_mask, NB + 1, axis=1), (9, 1))
    return jnp.where(wide_mask > 0, spline_coef, jnp.zeros_like(spline_coef))


def expand_bases(padded):
    values = padded.astype(jnp.float32)[:, None]
    centers = jnp.linspace(-2.0, 2.0, NB).astype(jnp.float32).reshape(1, NB, 1, 1, 1)
    spread = 4.0 / (NB - 1)
    bumps = jnp.exp(-jnp.square((values - centers) / spread))
    stacked = jnp.concatenate([bumps, jax.nn.silu(values)], axis=1)
    return stacked.astype(jnp.bfloat16).reshape(C * (NB + 1), -1)


def closure_band(padded, weight, rows, cols):
    table = expand_bases(padded)
    mixed = jnp.dot(weight, table, preferred_element_type=jnp.float32)
    mixed = mixed.reshape(9, C, L, rows + 2, cols + 2)
    total = jnp.zeros((C, L, rows, cols), jnp.float32)
    for offset in range(9):
        row_off, col_off = divmod(offset, 3)
        total = total + mixed[offset, :, :, row_off : row_off + rows, col_off : col_off + cols]
    return total


def feature_fold(top_row):
    count = lax.axis_size("lon")
    width = top_row.shape[-1]
    span = -(-width // count)
    extra = span * count - width
    spread = jnp.pad(top_row, ((0, 0), (0, 0), (0, extra)))
    spread = spread.reshape(top_row.shape[0], top_row.shape[1], count, span)
    spread = lax.all_to_all(spread, "lon", split_axis=2, concat_axis=2, tiled=True)
    spread = lax.all_to_all(spread[:, :, ::-1], "lon", split_axis=2, concat_axis=2, tiled=True)
    picked = spread.reshape(top_row.shape[0], top_row.shape[1], count * span)[..., :width]
    return picked[..., ::-1]


def surface_fold(top_row):
    count = lax.axis_size("lon")
    width = top_row.shape[0]
    span = -(-width // count)
    spread = top_row.reshape(count, span)
    spread = lax.all_to_all(spread, "lon", split_axis=0, concat_axis=0, tiled=True)
    spread = lax.all_to_all(spread[::-1], "lon", split_axis=0, concat_axis=0, tiled=True)
    picked = spread.reshape(count * span)
    return picked[::-1]


def operate(field, ocean, shift_coef):
    band_index = lax.axis_index("lat")
    band_count = lax.axis_size("lat")
    masked = ocean * field
    padded = extended(masked, (("lat", 0), ("lon", 1)), 1)
    folded = surface_fold(masked[-1])
    below = jnp.where(band_index == 0, jnp.zeros_like(padded[0, 1:-1]), padded[0, 1:-1])
    above = jnp.where(band_index == band_count - 1, folded, padded[-1, 1:-1])
    south = jnp.concatenate([below[None], masked[:-1]], axis=0)
    north = jnp.concatenate([masked[1:], above[None]], axis=0)
    west = padded[1:-1, :-2]
    east = padded[1:-1, 2:]
    return (
        ocean * ((4.0 + shift_coef) * field - (west + east + south + north)) + (1.0 - ocean) * field
    )


def body(features, spline_coef, edge_mask, head_weight, land_mask, shift_coef):
    band_index = lax.axis_index("lat")
    band_count = lax.axis_size("lat")
    weight = masked_weight(spline_coef, edge_mask)
    padded = extended(features, (("lat", 2), ("lon", 3)), 1)
    folded = feature_fold(padded[:, :, -2, :])
    below = jnp.where(band_index == 0, jnp.zeros_like(padded[:, :, 0]), padded[:, :, 0])
    above = jnp.where(band_index == band_count - 1, folded, padded[:, :, -1])
    padded = jnp.concatenate([below[:, :, None], padded[:, :, 1:-1], above[:, :, None]], axis=2)
    rows = features.shape[2]
    cols = features.shape[3]
    hidden = closure_band(padded, weight, rows, cols).astype(jnp.bfloat16)
    ocean = land_mask.astype(jnp.float32)
    mixed = jnp.dot(head_weight, hidden.reshape(C, -1), preferred_element_type=jnp.float32)
    tendency = (mixed.reshape(2, L, rows, cols) * ocean).astype(jnp.bfloat16)
    tend_f = tendency.astype(jnp.float32)
    west_col = passed_along(tendency[0, :, :, -1], "lon", 1).astype(jnp.float32)
    south_line = passed_along_2(tendency[1, :, -1, :], "lat", 1).astype(jnp.float32)
    west = jnp.concatenate([west_col[:, :, None], tend_f[0, :, :, :-1]], axis=2)
    south = jnp.concatenate([south_line[:, None, :], tend_f[1, :, :-1, :]], axis=1)
    rhs = ocean * jnp.sum(tend_f[0] - west + tend_f[1] - south, axis=0)
    surface = jnp.zeros_like(rhs)
    residual = rhs
    direction = rhs
    norm_now = lax.psum(jnp.sum(rhs * rhs), ("lon", "lat"))
    for step in range(ITERS):
        image = operate(direction, ocean, shift_coef)
        alpha = norm_now / lax.psum(jnp.sum(direction * image), ("lon", "lat"))
        surface = surface + alpha * direction
        residual = residual - alpha * image
        if step + 1 < ITERS:
            norm_next = lax.psum(jnp.sum(residual * residual), ("lon", "lat"))
            direction = residual + norm_next / norm_now * direction
            norm_now = norm_next
    return (tendency, surface, residual)


def solution(mesh):
    in_specs = (P(None, None, "lat", "lon"), P(), P(), P(), P("lat", "lon"), P("lat", "lon"))
    out_specs = (P(None, None, "lat", "lon"), P("lat", "lon"), P("lat", "lon"))
    return jax.shard_map(body, mesh=mesh, in_specs=in_specs, out_specs=out_specs, check_vma=False)
```

profile of v0, /device:TPU:1, one launch (start us, length us, event | category | flops | bytes accessed | tf_op | source)
XLA Modules:
  0.0 451.0 jit_solution(6045529079782050899)
XLA Ops:
  0.7 1.7 fusion.33
  2.5 2.2 collective-permute-start
  4.7 5.4 %collective-permute-start.1 = (bf16[48,2,1,512]{3,0,2,1:T(8,128)(2,1)S(1)}, bf16[48,2,1,512]{3,0,2,1:T(8,128)(2,1)S(1)}, u32[]{:S(2)}, u32[]{:S(2)}) collective-permute-start(bf16[48,2,1,512]{3,0,2,1:T(8,128)(2,1)S(1)} %copy.56), channel_id=1, source_target_pairs={{1,0},{2,1},{3,2},{4,3},{5,4},{6,5},{7,6},{8,7},{9,8},{10,9},{11,1... | collective-permute-start | bytes 294920 | tf_op jit(solution)/shard_map/ppermute | solution.py:21
  10.1 0.7 broadcast_compare_fusion
  10.8 1.6 collective-permute-done
  12.5 1.6 constant_dynamic-update-slice_fusion.1
  14.2 2.4 collective-permute-start.2
  17.1 0.6 convert_element_type.41
  17.7 0.8 bitcast_select_fusion
  18.5 1.3 collective-permute-done.2
  19.8 2.8 collective-permute-done.3
  22.5 0.8 maximum_select_fusion
  23.8 1.0 reshape.189
  24.9 8.9 %all-to-all-start = ((bf16[16,2,1584]{2,1,0:T(2,128)(2,1)}), bf16[16,2,1584]{2,1,0:T(2,128)(2,1)S(1)}, u32[]{:S(2)}, u32[]{:S(2)}) async-start(bf16[16,2,1584]{2,1,0:T(2,128)(2,1)} %reshape.189), calls=%async_computation | async-start | bytes 212992 | tf_op jit(solution)/shard_map/all_to_all | solution.py:70
  33.7 0.7 pad_maximum_fusion.1
  34.5 6.6 %all-to-all-done = bf16[16,2,1584]{2,1,0:T(2,128)(2,1)S(1)} async-done(((bf16[16,2,1584]{2,1,0:T(2,128)(2,1)}), bf16[16,2,1584]{2,1,0:T(2,128)(2,1)S(1)}, u32[]{:S(2)}, u32[]{:S(2)}) %all-to-all-start) | async-done | bytes 101408 | tf_op jit(solution)/shard_map/all_to_all | solution.py:70
  41.6 1.0 reshape.191
  42.6 3.9 all-to-all-start.1
  46.5 1.1 fusion.31
  47.6 6.3 %all-to-all-done.1 = bf16[16,2,1584]{2,1,0:T(2,128)(2,1)S(1)} async-done(((bf16[16,2,1584]{2,1,0:T(2,128)(2,1)}), bf16[16,2,1584]{2,1,0:T(2,128)(2,1)S(1)}, u32[]{:S(2)}, u32[]{:S(2)}) %all-to-all-start.1) | async-done | bytes 101408 | tf_op jit(solution)/shard_map/all_to_all | solution.py:71
  54.6 0.5 reverse
  55.1 0.9 fusion.5
  56.3 0.9 copy.37
  57.4 0.7 fusion.3
  58.5 7.1 %exponential_convert_fusion = bf16[48,9,2,10,514]{4,3,2,1,0:T(8,128)(2,1)S(1)} fusion(f32[9]{0:T(128)S(1)} %pad_maximum_fusion.20, f32[48,2,10,514]{3,2,1,0:T(8,128)S(1)} %copy.37), kind=kLoop, calls=%fused_computation | loop fusion | flops 22204800 | bytes 10855716 | tf_op jit(solution)/shard_map/convert.2
  65.6 9.8 %pad_maximum_fusion = bf16[48,10,2,10,514]{4,3,2,1,0:T(8,128)(2,1)} fusion(bf16[48,1,2,10,514]{4,3,2,1,0:T(8,128)(2,1)S(1)} %copy.38, bf16[48,9,2,10,514]{4,3,2,1,0:T(8,128)(2,1)S(1)} %exponential_convert_fusion), kind=kLoop, calls=%fused_computation.1 | loop fusion | flops 4934400 | bytes 19737600 | tf_op jit(solution)/shard_map/concatenate | solution.py:48
  75.4 24.5 %convert_element_type.39 = bf16[480,10280]{1,0:T(8,128)(2,1)} reshape(bf16[48,10,2,10,514]{4,3,2,1,0:T(8,128)(2,1)} %pad_maximum_fusion) | data formatting | bytes 19737600 | tf_op jit(solution)/shard_map/convert_element_type | solution.py:49
  100.0 14.3 %copy.39 = bf16[10280,480]{1,0:T(8,128)(2,1)} copy(bf16[10280,480]{0,1:T(8,128)(2,1)} %bitcast.84) | data formatting | bytes 19737600 | tf_op jit(solution)/shard_map/dot_general | solution.py:54
  114.2 11.4 %reshape.160 = bf16[2,10,514,480,1]{3,2,1,0,4:T(8,128)(2,1)} reshape(bf16[10280,480]{1,0:T(8,128)(2,1)} %copy.39) | data formatting | bytes 19737600 | tf_op jit(solution)/shard_map/dot_general | solution.py:54
  125.6 15.6 %fusion.38 = f32[9,48,2,10,514]{4,1,3,2,0:T(8,128)} fusion(bf16[9,48,480,1,1]{2,1,4,3,0:T(8,128)(2,1)S(1)} %bitcast.92, bf16[2,10,514,480,1]{3,2,1,0,4:T(8,128)(2,1)} %reshape.160), kind=kOutput, calls=%fused_computation.105 | convolution fusion | flops 4263321600 | bytes 28047360 | tf_op jit(solution)/shard_map/dot_general | solution.py:54
  141.2 8.3 %fusion.4 = bf16[1,48,2,8,512]{4,1,3,2,0:T(8,128)(2,1)S(1)} fusion(f32[9,48,2,10,514]{4,1,3,2,0:T(8,128)} %fusion.38), kind=kLoop, calls=%fused_computation.9 | loop fusion | flops 3538944 | bytes 14942208 | tf_op jit(solution)/shard_map/convert_element_type | solution.py:115
  149.6 0.4 copy.40
  150.0 0.4 reshape.158
  150.8 1.3 collective-permute-start.5
  152.1 0.6 collective-permute-start.4
  152.8 0.7 collective-permute-done.4
  153.7 1.0 collective-permute-start.6
  154.8 2.9 collective-permute-start.7
  157.6 0.7 all_to_all.36
  158.3 9.5 %all-to-all-start.2 = ((f32[16,1,32]{2,1,0:T(1,128)}), f32[16,1,32]{2,1,0:T(1,128)S(1)}, u32[]{:S(2)}, u32[]{:S(2)}) async-start(f32[16,1,32]{2,1,0:T(1,128)} %all_to_all.36), calls=%async_computation.2 | async-start | bytes 16384 | tf_op jit(solution)/shard_map/all_to_all | solution.py:81
  167.8 7.0 %all-to-all-done.2 = f32[16,1,32]{2,1,0:T(1,128)S(1)} async-done(((f32[16,1,32]{2,1,0:T(1,128)}), f32[16,1,32]{2,1,0:T(1,128)S(1)}, u32[]{:S(2)}, u32[]{:S(2)}) %all-to-all-start.2) | async-done | bytes 2080 | tf_op jit(solution)/shard_map/all_to_all | solution.py:81
  174.8 0.6 rev.20
  175.4 3.9 all-to-all-start.3
  179.4 1.7 collective-permute-start.8
  181.1 5.2 %all-to-all-done.3 = f32[16,1,32]{2,1,0:T(1,128)S(1)} async-done(((f32[16,1,32]{2,1,0:T(1,128)}), f32[16,1,32]{2,1,0:T(1,128)S(1)}, u32[]{:S(2)}, u32[]{:S(2)}) %all-to-all-start.3) | async-done | bytes 2080 | tf_op jit(solution)/shard_map/all_to_all | solution.py:82
  186.3 0.5 broadcast.77
  186.8 0.7 reduce.16
  187.7 0.8 multiply_reduce_fusion.2
  188.4 77.4 %all-reduce.1 = (f32[]{:T(128)}, f32[]{:T(128)}) all-reduce(f32[]{:T(128)} %get-tuple-element.4, f32[]{:T(128)} %get-tuple-element.3), channel_id=1, replica_groups=mesh['lon'=16,'lat'=16] {'lon','lat'}, use_global_device_ids=true, to_apply=%region_2.3 | all-reduce | flops 2 | bytes 16 | tf_op jit(solution)/shard_map/psum | solution.py:128
  267.2 0.6 multiply_reduce_fusion.1
  267.8 74.8 %psum.30 = f32[]{:T(128)} all-reduce(f32[]{:T(128)} %multiply_reduce_fusion.1), channel_id=1, replica_groups=mesh['lon'=16,'lat'=16] {'lon','lat'}, use_global_device_ids=true, to_apply=%region_6.7 | all-reduce | flops 1 | bytes 8 | tf_op jit(solution)/shard_map/psum | solution.py:135
  344.0 1.2 collective-permute-start.10
  345.1 2.5 collective-permute-start.11
  347.6 0.7 all_to_all.41
  348.3 5.4 %all-to-all-start.4 = ((f32[16,1,32]{2,1,0:T(1,128)}), f32[16,1,32]{2,1,0:T(1,128)S(1)}, u32[]{:S(2)}, u32[]{:S(2)}) async-start(f32[16,1,32]{2,1,0:T(1,128)} %all_to_all.41), calls=%async_computation.4 | async-start | bytes 16384 | tf_op jit(solution)/shard_map/all_to_all | solution.py:81
  353.7 6.9 %all-to-all-done.4 = f32[16,1,32]{2,1,0:T(1,128)S(1)} async-done(((f32[16,1,32]{2,1,0:T(1,128)}), f32[16,1,32]{2,1,0:T(1,128)S(1)}, u32[]{:S(2)}, u32[]{:S(2)}) %all-to-all-start.4) | async-done | bytes 2080 | tf_op jit(solution)/shard_map/all_to_all | solution.py:81
  360.6 0.6 rev.22
  361.2 3.9 all-to-all-start.5
  365.2 1.7 collective-permute-start.12
  366.9 5.2 %all-to-all-done.5 = f32[16,1,32]{2,1,0:T(1,128)S(1)} async-done(((f32[16,1,32]{2,1,0:T(1,128)}), f32[16,1,32]{2,1,0:T(1,128)S(1)}, u32[]{:S(2)}, u32[]{:S(2)}) %all-to-all-start.5) | async-done | bytes 2080 | tf_op jit(solution)/shard_map/all_to_all | solution.py:82
  372.1 0.7 reduce.17
  373.0 0.7 multiply_reduce_fusion
  373.7 75.4 %psum.31 = f32[]{:T(128)} all-reduce(f32[]{:T(128)} %get-tuple-element.7), channel_id=1, replica_groups=mesh['lon'=16,'lat'=16] {'lon','lat'}, use_global_device_ids=true, to_apply=%region_8.9 | all-reduce | flops 1 | bytes 8 | tf_op jit(solution)/shard_map/psum | solution.py:131
  450.4 0.6 multiply_subtract_fusion
  (83 shorter events, 4.4 us)
Async XLA Ops:
  0.6 149.7 %copy-start = (bf16[2,48]{1,0:T(2,128)(2,1)S(1)}, bf16[2,48]{1,0:T(2,128)(2,1)}, u32[]{:S(2)}) copy-start(bf16[2,48]{1,0:T(2,128)(2,1)} %param.9) | copy-start | bytes 580
  0.6 16.4 %copy-start.6 = (s32[8,512]{1,0:T(8,128)S(1)}, s32[8,512]{1,0:T(8,128)}, u32[]{:S(2)}) copy-start(s32[8,512]{1,0:T(8,128)} %param.10) | copy-start | bytes 49156
  0.7 17.0 %copy-start.4 = (bf16[432,480]{1,0:T(8,128)(2,1)S(1)}, bf16[432,480]{1,0:T(8,128)(2,1)}, u32[]{:S(2)}) copy-start(bf16[432,480]{1,0:T(8,128)(2,1)} %param.7) | copy-start | bytes 1244164
  2.5 10.0 %collective-permute-start = (bf16[48,2,1,512]{3,0,2,1:T(8,128)(2,1)S(1)}, bf16[48,2,1,512]{3,0,2,1:T(8,128)(2,1)S(1)}, u32[]{:S(2)}, u32[]{:S(2)}) collective-permute-start(bf16[48,2,1,512]{3,0,2,1:T(8,128)(2,1)S(1)} %copy.55), channel_id=1, source_target_pairs={{0,1},{1,2},{2,3},{3,4},{4,5},{5,6},{6,7},{7,8},{8,9},{9,10},{10,1... | collective-permute-start | bytes 294920 | tf_op jit(solution)/shard_map/ppermute | solution.py:18
  4.7 9.4 %collective-permute-start.1 = (bf16[48,2,1,512]{3,0,2,1:T(8,128)(2,1)S(1)}, bf16[48,2,1,512]{3,0,2,1:T(8,128)(2,1)S(1)}, u32[]{:S(2)}, u32[]{:S(2)}) collective-permute-start(bf16[48,2,1,512]{3,0,2,1:T(8,128)(2,1)S(1)} %copy.56), channel_id=1, source_target_pairs={{1,0},{2,1},{3,2},{4,3},{5,4},{6,5},{7,6},{8,7},{9,8},{10,9},{11,1... | collective-permute-start | bytes 294920 | tf_op jit(solution)/shard_map/ppermute | solution.py:21
  14.2 5.5 %collective-permute-start.2 = (bf16[48,2,10,1]{3,0,2,1:T(8,128)(2,1)S(1)}, bf16[48,2,10,1]{3,0,2,1:T(8,128)(2,1)S(1)}, u32[]{:S(2)}, u32[]{:S(2)}) collective-permute-start(bf16[48,2,10,1]{3,0,2,1:T(8,128)(2,1)S(1)} %get-tuple-element.18), channel_id=1, source_target_pairs={{0,16},{16,32},{32,48},{48,64},{64,80},{80,96},{96,112},{112,128},... | collective-permute-start | bytes 5768 | tf_op jit(solution)/shard_map/ppermute | solution.py:18
  16.6 5.9 %collective-permute-start.3 = (bf16[48,2,10,1]{3,0,2,1:T(8,128)(2,1)S(1)}, bf16[48,2,10,1]{3,0,2,1:T(8,128)(2,1)S(1)}, u32[]{:S(2)}, u32[]{:S(2)}) collective-permute-start(bf16[48,2,10,1]{3,0,2,1:T(8,128)(2,1)S(1)} %get-tuple-element.19), channel_id=1, source_target_pairs={{16,0},{32,16},{48,32},{64,48},{80,64},{96,80},{112,96},{128,112},... | collective-permute-start | bytes 5768 | tf_op jit(solution)/shard_map/ppermute | solution.py:21
  22.5 11.9 %copy-start.2 = (bf16[48,2,10,1]{3,0,2,1:T(8,128)(2,1)}, bf16[48,2,10,1]{3,0,2,1:T(8,128)(2,1)S(1)}, u32[]{:S(2)}) copy-start(bf16[48,2,10,1]{3,0,2,1:T(8,128)(2,1)S(1)} %collective-permute-done.3) | copy-start | bytes 5764
  24.9 16.2 %all-to-all-start = ((bf16[16,2,1584]{2,1,0:T(2,128)(2,1)}), bf16[16,2,1584]{2,1,0:T(2,128)(2,1)S(1)}, u32[]{:S(2)}, u32[]{:S(2)}) async-start(bf16[16,2,1584]{2,1,0:T(2,128)(2,1)} %reshape.189), calls=%async_computation | async-start | bytes 212992 | tf_op jit(solution)/shard_map/all_to_all | solution.py:70
  42.6 11.3 %all-to-all-start.1 = ((bf16[16,2,1584]{2,1,0:T(2,128)(2,1)}), bf16[16,2,1584]{2,1,0:T(2,128)(2,1)S(1)}, u32[]{:S(2)}, u32[]{:S(2)}) async-start(bf16[16,2,1584]{2,1,0:T(2,128)(2,1)} %reshape.191), calls=%async_computation.1 | async-start | bytes 212992 | tf_op jit(solution)/shard_map/all_to_all | solution.py:71
  47.6 8.4 %copy-start.3 = (bf16[48,2,1,514]{3,0,2,1:T(8,128)(2,1)S(1)}, bf16[48,2,1,514]{3,0,2,1:T(8,128)(2,1)}, u32[]{:S(2)}) copy-start(bf16[48,2,1,514]{3,0,2,1:T(8,128)(2,1)} %get-tuple-element.14) | copy-start | bytes 296068
  56.2 1.2 copy-start.1
  114.2 11.4 %copy-start.5 = (bf16[432,480]{1,0:T(8,128)(2,1)S(1)}, bf16[432,480]{1,0:T(8,128)(2,1)}, u32[]{:S(2)}) copy-start(bf16[432,480]{1,0:T(8,128)(2,1)} %bitcast_select_fusion) | copy-start | bytes 1244164
  149.5 1.1 copy-start.9
  149.5 4.2 copy-start.7
  149.5 38.1 %copy-start.8 = (f32[8,512]{1,0:T(8,128)S(1)}, f32[8,512]{1,0:T(8,128)}, u32[]{:S(2)}) copy-start(f32[8,512]{1,0:T(8,128)} %param.11) | copy-start | bytes 49156
  150.6 300.4 %copy-start.10 = (bf16[2,2,8,512]{3,2,1,0:T(8,128)(2,1)}, bf16[2,2,8,512]{3,2,1,0:T(8,128)(2,1)S(1)}, u32[]{:S(2)}) copy-start(bf16[2,2,8,512]{3,2,1,0:T(8,128)(2,1)S(1)} %get-tuple-element.13) | copy-start | bytes 98308
  150.8 2.7 collective-permute-start.5
  152.1 1.4 collective-permute-start.4
  153.7 25.6 %collective-permute-start.6 = (f32[1,512]{1,0:T(1,128)S(1)}, f32[1,512]{1,0:T(1,128)S(1)}, u32[]{:S(2)}, u32[]{:S(2)}) collective-permute-start(f32[1,512]{1,0:T(1,128)S(1)} %get-tuple-element.33), channel_id=1, source_target_pairs={{0,1},{1,2},{2,3},{3,4},{4,5},{5,6},{6,7},{7,8},{8,9},{9,10},{10,1... | collective-permute-start | bytes 6152 | tf_op jit(solution)/shard_map/ppermute | solution.py:18
  154.8 24.5 %collective-permute-start.7 = (f32[1,512]{1,0:T(1,128)S(1)}, f32[1,512]{1,0:T(1,128)S(1)}, u32[]{:S(2)}, u32[]{:S(2)}) collective-permute-start(f32[1,512]{1,0:T(1,128)S(1)} %get-tuple-element.35), channel_id=1, source_target_pairs={{1,0},{2,1},{3,2},{4,3},{5,4},{6,5},{7,6},{8,7},{9,8},{10,9},{11,1... | collective-permute-start | bytes 6152 | tf_op jit(solution)/shard_map/ppermute | solution.py:21
  158.3 16.4 %all-to-all-start.2 = ((f32[16,1,32]{2,1,0:T(1,128)}), f32[16,1,32]{2,1,0:T(1,128)S(1)}, u32[]{:S(2)}, u32[]{:S(2)}) async-start(f32[16,1,32]{2,1,0:T(1,128)} %all_to_all.36), calls=%async_computation.2 | async-start | bytes 16384 | tf_op jit(solution)/shard_map/all_to_all | solution.py:81
  175.4 10.9 %all-to-all-start.3 = ((f32[16,1,32]{2,1,0:T(1,128)}), f32[16,1,32]{2,1,0:T(1,128)S(1)}, u32[]{:S(2)}, u32[]{:S(2)}) async-start(f32[16,1,32]{2,1,0:T(1,128)} %bitcast.23), calls=%async_computation.3 | async-start | bytes 16384 | tf_op jit(solution)/shard_map/all_to_all | solution.py:82
  179.4 8.3 %collective-permute-start.8 = (f32[10,1]{1,0:T(8,128)S(1)}, f32[10,1]{1,0:T(8,128)S(1)}, u32[]{:S(2)}, u32[]{:S(2)}) collective-permute-start(f32[10,1]{1,0:T(8,128)S(1)} %get-tuple-element.26), channel_id=1, source_target_pairs={{0,16},{16,32},{32,48},{48,64},{64,80},{80,96},{96,112},{112,128},... | collective-permute-start | bytes 128 | tf_op jit(solution)/shard_map/ppermute | solution.py:18
  181.1 6.6 %collective-permute-start.9 = (f32[10,1]{1,0:T(8,128)S(1)}, f32[10,1]{1,0:T(8,128)S(1)}, u32[]{:S(2)}, u32[]{:S(2)}) collective-permute-start(f32[10,1]{1,0:T(8,128)S(1)} %get-tuple-element.27), channel_id=1, source_target_pairs={{16,0},{32,16},{48,32},{64,48},{80,64},{96,80},{112,96},{128,112},... | collective-permute-start | bytes 128 | tf_op jit(solution)/shard_map/ppermute | solution.py:21
  344.0 21.2 %collective-permute-start.10 = (f32[1,512]{1,0:T(1,128)S(1)}, f32[1,512]{1,0:T(1,128)S(1)}, u32[]{:S(2)}, u32[]{:S(2)}) collective-permute-start(f32[1,512]{1,0:T(1,128)S(1)} %get-tuple-element.28), channel_id=1, source_target_pairs={{0,1},{1,2},{2,3},{3,4},{4,5},{5,6},{6,7},{7,8},{8,9},{9,10},{10,1... | collective-permute-start | bytes 6152 | tf_op jit(solution)/shard_map/ppermute | solution.py:18
  345.1 20.0 %collective-permute-start.11 = (f32[1,512]{1,0:T(1,128)S(1)}, f32[1,512]{1,0:T(1,128)S(1)}, u32[]{:S(2)}, u32[]{:S(2)}) collective-permute-start(f32[1,512]{1,0:T(1,128)S(1)} %get-tuple-element.30), channel_id=1, source_target_pairs={{1,0},{2,1},{3,2},{4,3},{5,4},{6,5},{7,6},{8,7},{9,8},{10,9},{11,1... | collective-permute-start | bytes 6152 | tf_op jit(solution)/shard_map/ppermute | solution.py:21
  348.3 12.3 %all-to-all-start.4 = ((f32[16,1,32]{2,1,0:T(1,128)}), f32[16,1,32]{2,1,0:T(1,128)S(1)}, u32[]{:S(2)}, u32[]{:S(2)}) async-start(f32[16,1,32]{2,1,0:T(1,128)} %all_to_all.41), calls=%async_computation.4 | async-start | bytes 16384 | tf_op jit(solution)/shard_map/all_to_all | solution.py:81
  361.2 10.9 %all-to-all-start.5 = ((f32[16,1,32]{2,1,0:T(1,128)}), f32[16,1,32]{2,1,0:T(1,128)S(1)}, u32[]{:S(2)}, u32[]{:S(2)}) async-start(f32[16,1,32]{2,1,0:T(1,128)} %bitcast.28), calls=%async_computation.5 | async-start | bytes 16384 | tf_op jit(solution)/shard_map/all_to_all | solution.py:82
  365.2 7.8 %collective-permute-start.12 = (f32[10,1]{1,0:T(8,128)S(1)}, f32[10,1]{1,0:T(8,128)S(1)}, u32[]{:S(2)}, u32[]{:S(2)}) collective-permute-start(f32[10,1]{1,0:T(8,128)S(1)} %get-tuple-element.24), channel_id=1, source_target_pairs={{0,16},{16,32},{32,48},{48,64},{64,80},{80,96},{96,112},{112,128},... | collective-permute-start | bytes 128 | tf_op jit(solution)/shard_map/ppermute | solution.py:18
  366.9 6.1 %collective-permute-start.13 = (f32[10,1]{1,0:T(8,128)S(1)}, f32[10,1]{1,0:T(8,128)S(1)}, u32[]{:S(2)}, u32[]{:S(2)}) collective-permute-start(f32[10,1]{1,0:T(8,128)S(1)} %get-tuple-element.25), channel_id=1, source_target_pairs={{16,0},{32,16},{48,32},{64,48},{80,64},{96,80},{112,96},{128,112},... | collective-permute-start | bytes 128 | tf_op jit(solution)/shard_map/ppermute | solution.py:21
where the time goes:
time: 453 us; the launch traced here: 451 us
  blocking collectives  228 us (50%)
  local copies, waits for them, and re-layouts  65.4 us (14%)
  starting transfers between devices  58.3 us (13%)
  waiting for transfers between devices  43.7 us (10%)
  other arithmetic  35.1 us (8%)
  matrix products  15.8 us (3%)
  between operations  4.97 us (1%)
    psum x1, blocking collectives, body(): norm_now = lax.psum(jnp.sum(rhs * rhs), ('lon', 'lat'))  77.4 us
    psum x1, blocking collectives, body(): alpha = norm_now / lax.psum(jnp.sum(direction * image), ('lon', 'lat'))  75.4 us
    psum x1, blocking collectives, body(): norm_next = lax.psum(jnp.sum(residual * residual), ('lon', 'lat'))  74.8 us
    dot_general x2, local copies, waits for them, and re-layouts, closure_band(): mixed = jnp.dot(weight, table, preferred_element_type=jnp.float32)  25.7 us
    convert_element_type x1, local copies, waits for them, and re-layouts, expand_bases(): return stacked.astype(jnp.bfloat16).reshape(C * (NB + 1), -1)  24.5 us
    dot_general x1, matrix products, closure_band(): mixed = jnp.dot(weight, table, preferred_element_type=jnp.float32)  15.6 us
    all_to_all x2, starting transfers between devices, surface_fold(): lax.all_to_all(spread, 'lon', split_axis=0, concat_axis=0, tiled=True)  14.9 us
    all_to_all x2, waiting for transfers between devices, surface_fold(): lax.all_to_all(spread, 'lon', split_axis=0, concat_axis=0, tiled=True)  13.9 us
  transfers between devices with their start and end apart: 20, of which 10 were waited for; matrix products, arithmetic and copies ran while one was open for 2% of the time, Pallas kernels for 0%

commit v1 on v0

v1 whole, which is shorter than its diff:
```python
import functools
import math

import jax
import jax.numpy as jnp
from jax import lax
from jax.experimental import pallas as pl
from jax.experimental.pallas import tpu as pltpu
from jax.sharding import PartitionSpec as P

C = 48
NB = 9
J = NB + 1
L = 2
ROWS = 8
COLS = 512
WIDE = COLS + 128
F32 = jnp.float32
BF16 = jnp.bfloat16
MESH = pl.DeviceIdType.MESH
LOG2E = math.log2(math.e)
LIFT = 29
GROUP = 16
GROUPS = C // GROUP


def iota(shape, axis):
    return lax.broadcasted_iota(jnp.int32, shape, axis)


def dot(a, b):
    return jnp.dot(a, b, preferred_element_type=F32)


def ones_where(cond):
    return jnp.where(cond, 1.0, 0.0).astype(BF16)


def fold_weights(coef_ref, edge_ref, head_ref, wt, top):
    channel, lane = iota((C, C * J), 0), iota((C, C * J), 1)
    spread = ones_where((lane >= channel * J) & (lane < channel * J + J))
    keep = dot(jnp.where(edge_ref[...] > 0, 1.0, 0.0).astype(BF16), spread).astype(BF16)
    o, q = iota((C, 9 * C), 0), iota((C, 9 * C), 1)
    offset = lax.shift_right_logical(q * 1366, 16)
    head = dot(head_ref[...], ones_where(q - offset * C == o))
    r, q = iota((24, 9 * C), 0), iota((24, 9 * C), 1)
    offset = lax.shift_right_logical(q * 1366, 16)
    head = jnp.where((r & 1) == 0, head[0:1], head[1:2])
    head = jnp.where(lax.shift_right_logical(r, 1) == offset, head, 0.0).astype(BF16)
    folded = jnp.zeros((24, C * J), F32)
    masked = [coef_ref[C * k : C * k + C, :] * keep for k in range(9)]
    folded = dot(head, jnp.concatenate(masked, axis=0))
    lane = iota((1, C * J), 1)
    j = lane - J * lax.shift_right_logical(lane * 6554, 16)
    scale = jnp.where((j == 0) | (j == 8), math.exp(-6.0), jnp.where((j == 2) | (j == 6), math.exp(6.0), 1.0))
    folded = (folded * scale).astype(BF16)
    q = iota((1, 64 * J), 1)
    source = jnp.where((q & 63) < C, (q & 63) * J + lax.shift_right_logical(q, 6), -1)
    folded = dot(folded, ones_where(iota((C * J, 64 * J), 0) == source)).astype(BF16)
    q = iota((1, 2 * C * ROWS), 1)
    second = jnp.where(q >= C * ROWS, 1, 0)
    source = second * 64 + lax.shift_right_logical(q - second * (C * ROWS), 3)
    expand = ones_where(iota((128, 2 * C * ROWS), 0) == source)
    y_out = iota((ROWS, 2 * C * ROWS), 0)
    y_in = iota((ROWS, 2 * C * ROWS), 1) & 7
    first_row, last_row = y_in[0:6] == 0, y_in[0:6] == 7
    pad = jnp.zeros((2, 2 * C * ROWS), F32)
    for pair in range(J // 2):
        g = dot(folded[:, 128 * pair : 128 * pair + 128], expand)
        tiles = []
        for k in range(6):
            tile = jnp.where(y_in == y_out - 1, g[k : k + 1], 0.0)
            tile = jnp.where(y_in == y_out, g[6 + k : 7 + k], tile)
            tiles.append(jnp.where(y_in == y_out + 1, g[12 + k : 13 + k], tile))
        mirrored = jnp.concatenate([g[16:18], g[14:16], g[12:14]], axis=0)
        above = jnp.where(top, mirrored, g[0:6])
        tiles += [jnp.where(first_row, g[12:18], 0.0), pad, jnp.where(last_row, above, 0.0), pad]
        block = jnp.concatenate(tiles, axis=0).astype(BF16)
        for half in range(2):
            j = 2 * pair + half
            for group in range(GROUPS):
                at = half * C * ROWS + group * 128
                wt[group, :, 128 * j : 128 * j + 128] = block[:, at : at + 128]


def basis(x):
    base = (x * x) * (-4.0 * LOG2E)
    outer = base + (LIFT - 9.0 * LOG2E)
    slope = x * (12.0 * LOG2E)
    step = x * (4.0 * LOG2E)
    up = jnp.exp2(step - LOG2E)
    down = jnp.exp2(-LOG2E - step)
    left = jnp.exp2(outer - slope)
    middle = jnp.exp2(base + float(LIFT))
    right = jnp.exp2(outer + slope)
    half = x * (0.5 * 2.0**LIFT)
    silu = half + half * jnp.tanh(x * 0.5)
    return [left * down, left, left * up, middle * down, middle, middle * up, right * down, right, right * up, silu]


def kernel(
    n_lon, n_lat,
    feat_hbm, coef_ref, edge_ref, head_ref, land_ref, shift_ref,
    tend_ref, surf_ref, res_ref,
    feat, wt, bases, acc,
    north_m, south_m, both_m, got_m, side_m,
    north_p, south_p, east_p, west_p, got_p, side_p,
    lon_sums, lat_sums,
    feat_sem, send_m, recv_m, send_p, recv_p, send_a, recv_a,
):
    lon, lat = lax.axis_index("lon"), lax.axis_index("lat")
    top, bottom = lat == n_lat - 1, lat == 0
    east, west = lax.rem(lon + 1, n_lon), lax.rem(lon + n_lon - 1, n_lon)
    mirror = n_lon - 1 - lon
    up_lat = jnp.where(top, lat, lat + 1)
    up_lon = jnp.where(top, mirror, lon)
    up_east = jnp.where(top, n_lon - 1 - east, east)
    up_west = jnp.where(top, n_lon - 1 - west, west)
    down_lat = jnp.where(bottom, lat, lat - 1)
    east_self = top & (up_east == lon)
    west_self = top & (up_west == lon)

    feat_in = [
        pltpu.make_async_copy(feat_hbm.at[:, level], feat.at[level], feat_sem.at[level]) for level in range(L)
    ]
    for copy in feat_in:
        copy.start()

    barrier = pltpu.get_barrier_semaphore()

    def greet(at_lon, at_lat):
        pl.semaphore_signal(barrier, inc=1, device_id={"lon": at_lon, "lat": at_lat}, device_id_type=MESH)

    for d in range(1, n_lon):
        greet(lax.rem(lon + d, n_lon), lat)
    for d in range(1, n_lat):
        greet(lon, lax.rem(lat + d, n_lat))

    @pl.when(jnp.logical_not(top))
    def _():
        greet(east, up_lat)
        greet(west, up_lat)

    @pl.when(jnp.logical_not(bottom))
    def _():
        greet(east, down_lat)
        greet(west, down_lat)

    def remote(src, dst, send, recv, at_lon, at_lat):
        return pltpu.make_async_remote_copy(
            src_ref=src, dst_ref=dst, send_sem=send, recv_sem=recv,
            device_id={"lon": at_lon, "lat": at_lat}, device_id_type=MESH,
        )

    class Exchange:
        def __init__(self, north, south, to_east, to_west, got, side, send, recv, whole, ne, nw):
            width = ne[1]
            mid = pl.ds(*whole)
            e, w = pl.ds(*ne), pl.ds(*nw)
            part = pl.ds(0, width)
            self.got, self.side = got, side
            base = jnp.where(top, 3, 0)
            self.local = [
                (east_self, got.at[4, :, part], north.at[:, e]),
                (west_self, got.at[5, :, part], north.at[:, w]),
            ]
            self.sends = [
                (None, remote(north.at[:, mid], got.at[base], send.at[0], recv.at[base], up_lon, up_lat)),
                (jnp.logical_not(east_self), remote(north.at[:, e], got.at[base + 1, :, part], send.at[1], recv.at[base + 1], up_east, up_lat)),
                (jnp.logical_not(west_self), remote(north.at[:, w], got.at[base + 2, :, part], send.at[2], recv.at[base + 2], up_west, up_lat)),
                (jnp.logical_not(bottom), remote(south.at[:, mid], got.at[3], send.at[3], recv.at[3], lon, down_lat)),
                (jnp.logical_not(bottom), remote(south.at[:, e], got.at[4, :, part], send.at[4], recv.at[4], east, down_lat)),
                (jnp.logical_not(bottom), remote(south.at[:, w], got.at[5, :, part], send.at[5], recv.at[5], west, down_lat)),
                (None, remote(to_east, side.at[0], send.at[6], recv.at[6], east, lat)),
                (None, remote(to_west, side.at[1], send.at[7], recv.at[7], west, lat)),
            ]
            corner = got.at[0, :, part]
            has_south = jnp.logical_not(bottom)

            def arrival(src, dst, k):
                return remote(src, dst, send.at[0], recv.at[k], east, lat)

            self.arrivals = [
                (has_south, arrival(north.at[:, mid], got.at[0], 0)),
                (has_south, arrival(north.at[:, e], got.at[1, :, part], 1)),
                (has_south, arrival(north.at[:, w], got.at[2, :, part], 2)),
                (None, arrival(north.at[:, mid], got.at[3], 3)),
                (jnp.logical_not(east_self), arrival(north.at[:, e], got.at[4, :, part], 4)),
                (jnp.logical_not(west_self), arrival(north.at[:, w], got.at[5, :, part], 5)),
                (None, arrival(to_east, side.at[0], 6)),
                (None, arrival(to_west, side.at[1], 7)),
            ]

        def each(self, entries, act):
            for cond, copy in entries:
                if cond is None:
                    act(copy)
                else:
                    pl.when(cond)(functools.partial(act, copy))

        def start(self):
            for cond, dst, src in self.local:
                def place(dst=dst, src=src):
                    dst[...] = src[...]

                pl.when(cond)(place)

            self.each(self.sends, lambda copy: copy.start())

        def arrive(self):
            self.each(self.arrivals, lambda copy: copy.wait_recv())

        def leave(self):
            self.each(self.sends, lambda copy: copy.wait_send())

    @pl.when(bottom)
    def _():
        got_m[0:3] = jnp.zeros((3,) + got_m.shape[1:], F32)
        got_p[0:3] = jnp.zeros((3,) + got_p.shape[1:], F32)

    ocean = land_ref[...].astype(F32)
    shift = shift_ref[...]
    both_m[0:8] = ocean
    both_m[8:16] = shift
    none = jnp.zeros((1, COLS), F32)
    north_m[...] = jnp.concatenate([ocean[7:8], shift[7:8]] + [none] * 6, axis=0)
    south_m[...] = jnp.concatenate([ocean[0:1], shift[0:1], ocean[1:2]] + [none] * 5, axis=0)

    fold_weights(coef_ref, edge_ref, head_ref, wt, top)

    diagonals = 4 - 2 * jnp.where(top | bottom, 1, 0)
    pl.semaphore_wait(barrier, n_lon + n_lat - 2 + diagonals)

    masks = Exchange(
        north_m, south_m, both_m.at[:, pl.ds(COLS - 128, 128)], both_m.at[:, pl.ds(0, 128)],
        got_m, side_m, send_m, recv_m, (0, COLS), (COLS - 128, 128), (0, 128),
    )
    masks.start()

    acc[...] = jnp.zeros(acc.shape, F32)
    for level in range(L):
        feat_in[level].wait()

        def step(group, carry):
            x = feat[level, pl.ds(group * GROUP, GROUP)].astype(F32).reshape(GROUP * ROWS, COLS)
            for j, value in enumerate(basis(x)):
                bases[128 * j : 128 * j + 128, :] = value.astype(BF16)
            acc[level, :, 0:COLS] += dot(wt[group], bases[...])
            return carry

        lax.fori_loop(0, GROUPS, step, 0)

    masks.arrive()

    lane = iota((ROWS, 128), 1)
    low = lane < 64
    row = iota((ROWS, WIDE), 0)
    backwards = 127 - lane

    def tiles_of(x):
        return [x[:, 128 * k : 128 * k + 128] for k in range(x.shape[1] // 128)]

    def flip(parts):
        turned = [jnp.take_along_axis(p, backwards, axis=1) for p in parts]
        return turned[3::-1] + turned[4:]

    def joined(parts):
        return jnp.concatenate(parts, axis=1)

    def from_north(parts):
        turned = flip(parts)
        return joined([jnp.where(top, b, a) for a, b in zip(parts, turned)])

    def mask_rows(k):
        parts = tiles_of(got_m[k])
        return parts + [jnp.where(low, got_m[k + 2, :, 0:128], got_m[k + 1, :, 0:128])]

    south_rows = joined(mask_rows(0))
    north_rows = from_north(mask_rows(3))
    side = jnp.where(
        jnp.concatenate([low, low], axis=0), side_m[1], side_m[0]
    )
    zero = jnp.zeros((ROWS, WIDE), F32)

    def extended(own, own_side, north1, north2, south1):
        outer = jnp.where(row == 0, north1, jnp.where(row == 1, north2, jnp.where(row == 7, south1, zero)))
        return jnp.concatenate([joined([own, own_side]), outer], axis=0)

    second = jnp.where(top, zero[0:1], north_rows[2:3])
    m = extended(ocean, side[0:8], north_rows[0:1], second, south_rows[0:1])
    s = extended(shift, side[8:16], north_rows[1:2], zero[0:1], south_rows[1:2])

    def lanes(x, by):
        return pltpu.roll(x, by % WIDE, 1)

    def rows(x, by):
        return pltpu.roll(x, by % 16, 0)

    own, above, below = [], [], []
    for level in range(L):
        a = acc[level] * (2.0**-LIFT)
        own.append(a[16:32] + lanes(a[0:16], 1) + lanes(a[32:48], -1))
        outer = a[48:64]
        before, after = lanes(outer, 1), lanes(outer, -1)
        below.append(outer[2:4] + before[0:2] + after[4:6])
        above.append(outer[10:12] + before[8:10] + after[12:14])
    j = lax.shift_right_logical(iota((1, 128 * J), 1), 7)
    off = jnp.abs(j - 4)
    still = jnp.where(off == 1, math.exp(-1.0), jnp.where(off == 2, math.exp(-10.0), jnp.where(off == 3, math.exp(-9.0), math.exp(-10.0))))
    still = jnp.where(off == 0, 1.0, jnp.where(j == NB, 0.0, still))
    outside = jnp.zeros((8, 128 * J), F32)
    for group in range(GROUPS):
        outside = outside + wt[group, 48:64, :].astype(F32)[8:16]
    outside = jnp.where(bottom, jnp.sum(outside * still, axis=1, keepdims=True), 0.0)
    first = (iota((8, WIDE), 0) == 0) & (iota((8, WIDE), 1) < COLS)
    for level in range(L):
        own[level] = jnp.concatenate(
            [own[level][8 * c : 8 * c + 8] + jnp.where(first, outside[c : c + 1] + outside[c + 2 : c + 3] + outside[c + 4 : c + 5], 0.0) for c in range(2)],
            axis=0,
        )
    total, total_up, total_down = own[0] + own[1], above[0] + above[1], below[0] + below[1]

    def field(c):
        outer = jnp.where(row == 0, total_up[c : c + 1], jnp.where(row == 7, total_down[c : c + 1], zero))
        return m * jnp.concatenate([total[8 * c : 8 * c + 8], outer], axis=0)

    eastward, northward = field(0), field(1)
    part = m * (eastward - lanes(eastward, 1) + northward - rows(northward, 1))
    folded = m[8:16] * (eastward[8:16] - lanes(eastward, -1)[8:16] + northward[8:16])
    part = jnp.concatenate([part[0:8], jnp.where(top & (row == 0), folded, part[8:16])], axis=0)

    edge_n = jnp.concatenate([part[8:9], part[7:8], part[6:7], part[9:10], above[0], above[1]], axis=0)
    edge_s = jnp.concatenate([part[15:16], part[0:1], part[1:2], zero[0:1], below[0], below[1]], axis=0)
    for edge, ref in ((edge_n, north_p), (edge_s, south_p)):
        ref[:, 0:128] = edge[:, COLS:]
        ref[:, 128:] = edge
    east_p[0:16, :] = part[:, COLS - 128 :]
    west_p[0:16, 0:128] = part[:, COLS:]
    west_p[0:16, 128:] = part[:, 0:128]
    for level in range(L):
        halo = own[level][:, COLS:]
        for ref in (east_p, west_p):
            ref[16:32, 128 * level : 128 * level + 128] = halo

    partials = Exchange(
        north_p, south_p, east_p, west_p,
        got_p, side_p, send_p, recv_p, (128, WIDE), (COLS, 256), (0, 256),
    )
    partials.start()
    partials.arrive()

    def part_rows(k):
        t = tiles_of(got_p[k])
        w, e = got_p[k + 1, :, 0:256], got_p[k + 2, :, 0:256]
        t[0] = t[0] + jnp.where(low, w[:, 128:], 0.0)
        t[3] = t[3] + jnp.where(low, 0.0, e[:, :128])
        t[4] = t[4] + jnp.where(low, e[:, 128:], w[:, :128])
        return t

    south_rows = joined(part_rows(0))
    north_rows = from_north(part_rows(3))
    from_west, from_east = side_p[0], side_p[1]
    low2 = jnp.concatenate([low, low], axis=0)

    inner = jnp.where(row == 0, south_rows[0:1], jnp.where(row == 1, south_rows[3:4], jnp.where(row == 7, north_rows[0:1], zero)))
    outer = jnp.where(row == 0, north_rows[1:2], jnp.where(row == 1, north_rows[2:3], jnp.where(row == 6, south_rows[2:3], jnp.where(row == 7, south_rows[1:2], zero))))
    r = part + jnp.concatenate([inner, outer], axis=0)
    r = joined([
        r[:, 0:128] + jnp.where(low2, from_west[0:16, 128:], 0.0),
        r[:, 128 : COLS - 128],
        r[:, COLS - 128 : COLS] + jnp.where(low2, 0.0, from_east[0:16, 0:128]),
        r[:, COLS:] + jnp.where(low2, from_east[0:16, 128:], from_west[0:16, 0:128]),
    ])

    def operate(v):
        return m * ((4.0 + s) * v - (lanes(v, 1) + lanes(v, -1) + rows(v, 1) + rows(v, -1)))

    q1 = operate(r)
    q2 = operate(q1)[0:8, 0:COLS]
    r, q1 = r[0:8, 0:COLS], q1[0:8, 0:COLS]

    def summed(x):
        x = x[:, 0:128] + x[:, 128:256] + x[:, 256:384] + x[:, 384:512]
        return jnp.sum(x, axis=0, keepdims=True)

    sums = [summed(r * r), summed(r * q1), summed(q1 * q1), summed(r * q2), summed(q1 * q2)]
    mine = jnp.concatenate(sums + [jnp.zeros((3, 128), F32)], axis=0)

    def all_sum(value, ref, stage, count, here, device):
        ref[here] = value
        out = []
        for d in range(1, count):
            there = lax.rem(here + d, count)
            copy = remote(ref.at[here], ref.at[here], send_a.at[stage, d], recv_a.at[stage, here], *device(there))
            copy.start()
            out.append(copy)
        for d in range(1, count):
            there = lax.rem(here + d, count)
            remote(ref.at[there], ref.at[there], send_a.at[stage, d], recv_a.at[stage, there], *device(there)).wait_recv()
        return jnp.sum(ref[...], axis=0), out

    value, copies_lon = all_sum(mine, lon_sums, 0, n_lon, lon, lambda k: (k, lat))
    value, copies_lat = all_sum(value, lat_sums, 1, n_lat, lat, lambda k: (lon, k))

    for level in range(L):
        for c in range(2):
            t = own[level][8 * c : 8 * c + 8]
            k = 4 + 2 * level + c
            t = t + jnp.where(row == 0, south_rows[k : k + 1], jnp.where(row == 7, north_rows[k : k + 1], zero))
            at = slice(128 * level, 128 * level + 128)
            w = jnp.where(lane == 0, from_west[16 + 8 * c : 24 + 8 * c, at], 0.0)
            e = jnp.where(lane == 127, from_east[16 + 8 * c : 24 + 8 * c, at], 0.0)
            t = joined([t[:, 0:128] + w, t[:, 128 : COLS - 128], t[:, COLS - 128 : COLS] + e])
            tend_ref[c, level] = (ocean * t).astype(BF16)

    value = jnp.sum(value, axis=1, keepdims=True)
    rr, rq, qq, rq2, qq2 = [value[k : k + 1] for k in range(5)]
    a1 = rr / rq
    new = rr - 2.0 * a1 * rq + a1 * a1 * qq
    lead = 1.0 + new / rr
    a2 = new / (lead * lead * rq - lead * a1 * (rq2 + qq) + a1 * a1 * qq2)
    surf_ref[...] = a1 * r + a2 * (lead * r - a1 * q1)
    res_ref[...] = r - a1 * q1 - a2 * (lead * q1 - a1 * q2)

    masks.leave()
    partials.leave()
    for copy in copies_lon + copies_lat:
        copy.wait_send()


def body(features, spline_coef, edge_mask, head_weight, land_mask, shift_coef):
    n_lon, n_lat = lax.axis_size("lon"), lax.axis_size("lat")
    vmem = pl.BlockSpec(memory_space=pltpu.VMEM)
    dma = pltpu.SemaphoreType.DMA
    scratch = [
        pltpu.VMEM((L, C, ROWS, COLS), BF16),
        pltpu.VMEM((GROUPS, 64, 128 * J), BF16),
        pltpu.VMEM((128 * J, COLS), BF16),
        pltpu.VMEM((L, 64, WIDE), F32),
        pltpu.VMEM((8, COLS), F32),
        pltpu.VMEM((8, COLS), F32),
        pltpu.VMEM((16, COLS), F32),
        pltpu.VMEM((6, 8, COLS), F32),
        pltpu.VMEM((2, 16, 128), F32),
        pltpu.VMEM((8, WIDE + 128), F32),
        pltpu.VMEM((8, WIDE + 128), F32),
        pltpu.VMEM((32, 256), F32),
        pltpu.VMEM((32, 256), F32),
        pltpu.VMEM((6, 8, WIDE), F32),
        pltpu.VMEM((2, 32, 256), F32),
        pltpu.VMEM((n_lon, 8, 128), F32),
        pltpu.VMEM((n_lat, 8, 128), F32),
        dma((L,)),
        dma((8,)), dma((8,)), dma((8,)), dma((8,)),
        dma((2, max(n_lon, n_lat))), dma((2, max(n_lon, n_lat))),
    ]
    return pl.pallas_call(
        functools.partial(kernel, n_lon, n_lat),
        out_shape=(
            jax.ShapeDtypeStruct((2, L, ROWS, COLS), BF16),
            jax.ShapeDtypeStruct((ROWS, COLS), F32),
            jax.ShapeDtypeStruct((ROWS, COLS), F32),
        ),
        in_specs=[pl.BlockSpec(memory_space=pl.ANY)] + [vmem] * 5,
        out_specs=(vmem, vmem, vmem),
        scratch_shapes=scratch,
        compiler_params=pltpu.CompilerParams(
            collective_id=0, has_side_effects=True, vmem_limit_bytes=48 * 1024 * 1024
        ),
        name="closure_and_cg",
    )(features, spline_coef, edge_mask, head_weight, land_mask, shift_coef)


def solution(mesh):
    in_specs = (P(None, None, "lat", "lon"), P(), P(), P(), P("lat", "lon"), P("lat", "lon"))
    out_specs = (P(None, None, "lat", "lon"), P("lat", "lon"), P("lat", "lon"))
    return jax.shard_map(body, mesh=mesh, in_specs=in_specs, out_specs=out_specs, check_vma=False)
```

time: 453 us -> 37.9 us (0.08)
  blocking collectives: 228 us -> 0 us
  local copies, waits for them, and re-layouts: 65.4 us -> 6.79 us
  starting transfers between devices: 58.3 us -> 0 us
  waiting for transfers between devices: 43.7 us -> 0 us
  other arithmetic: 35.1 us -> 0 us
  Pallas kernels: 0 us -> 30.2 us
  matrix products: 15.8 us -> 0 us
    psum x3 -> x0, blocking collectives: 228 us -> none  [the longest x1 77.4 us: body(): norm_now = lax.psum(jnp.sum(rhs * rhs), ('lon', 'lat'))]
    all_to_all x6 -> x0, waiting for transfers between devices: 37.3 us -> none  [the longest x2 13.9 us: surface_fold(): lax.all_to_all(spread, 'lon', split_axis=0, concat_axis=0, tiled=True)]
    all_to_all x6 -> x0, starting transfers between devices: 35.5 us -> none  [the longest x2 14.9 us: surface_fold(): lax.all_to_all(spread, 'lon', split_axis=0, concat_axis=0, tiled=True)]
    pallas_call x0 -> x1, Pallas kernels: none -> 30.2 us  [body(): pl.pallas_call(functools.partial(kernel, n_lon, n_lat), out_shape=(jax.Sh...]
    convert_element_type x4 -> x0, local copies, waits for them, and re-layouts: 26.2 us -> none  [the longest x1 24.5 us: expand_bases(): return stacked.astype(jnp.bfloat16).reshape(C * (NB + 1), -1)]
    dot_general x2 -> x0, local copies, waits for them, and re-layouts: 25.7 us -> none  [closure_band(): mixed = jnp.dot(weight, table, preferred_element_type=jnp.float32)]
    ppermute x14 -> x0, starting transfers between devices: 22.8 us -> none  [the longest x6 10.8 us: extended(): lax.ppermute(lax.slice_in_dim(block, 0, width, axis=dim), axis, backward)]
    dot_general x2 -> x0, matrix products: 15.8 us -> none  [the longest x1 15.6 us: closure_band(): mixed = jnp.dot(weight, table, preferred_element_type=jnp.float32)]
  transfers between devices with their start and end apart: 20 -> 0, of which waited for: 10 -> 0; matrix products, arithmetic and copies ran while one was open for 2% -> 0% of each run, Pallas kernels for 0% -> 0%
where the time goes in v1:
time: 37.9 us; the launch traced here: 37.6 us
  Pallas kernels  30.2 us (80%)
  local copies, waits for them, and re-layouts  6.79 us (18%)
  between operations  0.65 us (2%)
    pallas_call x1, Pallas kernels, body(): pl.pallas_call(functools.partial(kernel, n_lon, n_lat), out_shape=(jax.Sh...  30.2 us
    unnamed x15, local copies, waits for them, and re-layouts  6.79 us

profile of v1, /device:TPU:1, one launch (start us, length us, event | category | flops | bytes accessed | tf_op | source)
XLA Modules:
  0.0 37.6 jit_solution(17182687604467580422)
XLA Ops:
  0.6 0.0 copy-start
  0.6 1.1 %copy-done = bf16[48,2,8,512]{3,2,1,0:T(8,128)(2,1)S(1)} copy-done((bf16[48,2,8,512]{3,2,1,0:T(8,128)(2,1)S(1)}, bf16[48,2,8,512]{3,2,1,0:T(8,128)(2,1)}, u32[]{:S(2)}) %copy-start) | copy-done | bytes 786456
  1.8 0.0 copy-start.1
  1.8 1.0 %copy-done.1 = bf16[432,480]{1,0:T(8,128)(2,1)S(1)} copy-done((bf16[432,480]{1,0:T(8,128)(2,1)S(1)}, bf16[432,480]{1,0:T(8,128)(2,1)}, u32[]{:S(2)}) %copy-start.1) | copy-done | bytes 414744
  2.8 0.0 copy-start.2
  2.8 0.7 %copy-done.2 = s32[48,48]{1,0:T(8,128)S(1)} copy-done((s32[48,48]{1,0:T(8,128)S(1)}, s32[48,48]{1,0:T(8,128)}, u32[]{:S(2)}) %copy-start.2) | copy-done | bytes 9240
  3.5 0.0 copy-start.3
  3.5 0.7 %copy-done.3 = s32[8,512]{1,0:T(8,128)S(1)} copy-done((s32[8,512]{1,0:T(8,128)S(1)}, s32[8,512]{1,0:T(8,128)}, u32[]{:S(2)}) %copy-start.3) | copy-done | bytes 16408
  4.2 0.0 copy-start.4
  4.2 0.7 %copy-done.4 = f32[8,512]{1,0:T(8,128)S(1)} copy-done((f32[8,512]{1,0:T(8,128)S(1)}, f32[8,512]{1,0:T(8,128)}, u32[]{:S(2)}) %copy-start.4) | copy-done | bytes 16408
  5.0 0.0 copy-start.5
  5.0 0.7 %copy-done.5 = bf16[2,48]{1,0:T(2,128)(2,1)S(1)} copy-done((bf16[2,48]{1,0:T(2,128)(2,1)S(1)}, bf16[2,48]{1,0:T(2,128)(2,1)}, u32[]{:S(2)}) %copy-start.5) | copy-done | bytes 216
  5.6 30.2 %closure_and_cg.1 = (bf16[2,2,8,512]{3,2,1,0:T(8,128)(2,1)S(1)}, f32[8,512]{1,0:T(8,128)S(1)}, f32[8,512]{1,0:T(8,128)S(1)}) custom-call(bf16[48,2,8,512]{3,2,1,0:T(8,128)(2,1)S(1)} %copy-done, bf16[432,480]{1,0:T(8,128)(2,1)S(1)} %copy-done.1, s32[48,48]{1,0:T(8,128)S(1)} %copy-done.2, bf16[2,48]{1,0:T(2,128)(2,1)S(1)} %copy-done.5, ...), custom_call_target="tpu_custom_call" | custom-call | tf_op jit(solution)/shard_map/closure_and_cg/pallas_call | solution.py:457
  35.8 0.6 %copy.12 = bf16[2,2,8,512]{3,2,1,0:T(8,128)(2,1)} copy(bf16[2,2,8,512]{3,2,1,0:T(8,128)(2,1)S(1)} %get-tuple-element.6) | data formatting | bytes 65536
  36.4 0.6 %copy.13 = f32[8,512]{1,0:T(8,128)} copy(f32[8,512]{1,0:T(8,128)S(1)} %get-tuple-element.7) | data formatting | bytes 32768
  37.0 0.6 %copy.14 = f32[8,512]{1,0:T(8,128)} copy(f32[8,512]{1,0:T(8,128)S(1)} %get-tuple-element.8) | data formatting | bytes 32768
Async XLA Ops:
  0.6 1.1 %copy-start = (bf16[48,2,8,512]{3,2,1,0:T(8,128)(2,1)S(1)}, bf16[48,2,8,512]{3,2,1,0:T(8,128)(2,1)}, u32[]{:S(2)}) copy-start(bf16[48,2,8,512]{3,2,1,0:T(8,128)(2,1)} %feat_hbm.1) | copy-start | bytes 2359300
  1.8 1.0 %copy-start.1 = (bf16[432,480]{1,0:T(8,128)(2,1)S(1)}, bf16[432,480]{1,0:T(8,128)(2,1)}, u32[]{:S(2)}) copy-start(bf16[432,480]{1,0:T(8,128)(2,1)} %coef_ref.1) | copy-start | bytes 1244164
  2.8 0.7 %copy-start.2 = (s32[48,48]{1,0:T(8,128)S(1)}, s32[48,48]{1,0:T(8,128)}, u32[]{:S(2)}) copy-start(s32[48,48]{1,0:T(8,128)} %edge_ref.1) | copy-start | bytes 27652
  3.5 0.7 %copy-start.3 = (s32[8,512]{1,0:T(8,128)S(1)}, s32[8,512]{1,0:T(8,128)}, u32[]{:S(2)}) copy-start(s32[8,512]{1,0:T(8,128)} %land_ref.1) | copy-start | bytes 49156
  4.2 0.7 %copy-start.4 = (f32[8,512]{1,0:T(8,128)S(1)}, f32[8,512]{1,0:T(8,128)}, u32[]{:S(2)}) copy-start(f32[8,512]{1,0:T(8,128)} %shift_ref.1) | copy-start | bytes 49156
  5.0 0.7 %copy-start.5 = (bf16[2,48]{1,0:T(2,128)(2,1)S(1)}, bf16[2,48]{1,0:T(2,128)(2,1)}, u32[]{:S(2)}) copy-start(bf16[2,48]{1,0:T(2,128)(2,1)} %head_ref.1) | copy-start | bytes 580

commit v2 on v1

v2 whole, which is shorter than its diff:
```python
import functools
import math

import jax
import jax.numpy as jnp
from jax import lax
from jax.experimental import pallas as pl
from jax.experimental.pallas import tpu as pltpu
from jax.sharding import PartitionSpec as P

C = 48
NB = 9
J = NB + 1
L = 2
ROWS = 8
COLS = 512
WIDE = COLS + 128
F32 = jnp.float32
BF16 = jnp.bfloat16
MESH = pl.DeviceIdType.MESH
LOG2E = math.log2(math.e)
LIFT = 29
GROUP = 16
GROUPS = C // GROUP
STRIP = 2


def iota(shape, axis):
    return lax.broadcasted_iota(jnp.int32, shape, axis)


def dot(a, b):
    return jnp.dot(a, b, preferred_element_type=F32)


def ones_where(cond):
    return jnp.where(cond, 1.0, 0.0).astype(BF16)


def fold_weights(coef_ref, edge_ref, head_ref, wt, top):
    channel, lane = iota((C, C * J), 0), iota((C, C * J), 1)
    spread = ones_where((lane >= channel * J) & (lane < channel * J + J))
    keep = dot(jnp.where(edge_ref[...] > 0, 1.0, 0.0).astype(BF16), spread).astype(BF16)
    o, q = iota((C, 9 * C), 0), iota((C, 9 * C), 1)
    offset = lax.shift_right_logical(q * 1366, 16)
    head = dot(head_ref[...], ones_where(q - offset * C == o))
    r, q = iota((24, 9 * C), 0), iota((24, 9 * C), 1)
    offset = lax.shift_right_logical(q * 1366, 16)
    head = jnp.where((r & 1) == 0, head[0:1], head[1:2])
    head = jnp.where(lax.shift_right_logical(r, 1) == offset, head, 0.0).astype(BF16)
    folded = jnp.zeros((24, C * J), F32)
    masked = [coef_ref[C * k : C * k + C, :] * keep for k in range(9)]
    folded = dot(head, jnp.concatenate(masked, axis=0))
    lane = iota((1, C * J), 1)
    j = lane - J * lax.shift_right_logical(lane * 6554, 16)
    scale = jnp.where((j == 0) | (j == 8), math.exp(-6.0), jnp.where((j == 2) | (j == 6), math.exp(6.0), 1.0))
    folded = (folded * scale).astype(BF16)
    q = iota((1, 64 * J), 1)
    source = jnp.where((q & 63) < C, (q & 63) * J + lax.shift_right_logical(q, 6), -1)
    folded = dot(folded, ones_where(iota((C * J, 64 * J), 0) == source)).astype(BF16)
    q = iota((1, 2 * C * ROWS), 1)
    second = jnp.where(q >= C * ROWS, 1, 0)
    source = second * 64 + lax.shift_right_logical(q - second * (C * ROWS), 3)
    expand = ones_where(iota((128, 2 * C * ROWS), 0) == source)
    y_out = iota((ROWS, 2 * C * ROWS), 0)
    y_in = iota((ROWS, 2 * C * ROWS), 1) & 7
    first_row, last_row = y_in[0:6] == 0, y_in[0:6] == 7
    pad = jnp.zeros((2, 2 * C * ROWS), F32)
    for pair in range(J // 2):
        g = dot(folded[:, 128 * pair : 128 * pair + 128], expand)
        tiles = []
        for k in range(6):
            tile = jnp.where(y_in == y_out - 1, g[k : k + 1], 0.0)
            tile = jnp.where(y_in == y_out, g[6 + k : 7 + k], tile)
            tiles.append(jnp.where(y_in == y_out + 1, g[12 + k : 13 + k], tile))
        mirrored = jnp.concatenate([g[16:18], g[14:16], g[12:14]], axis=0)
        above = jnp.where(top, mirrored, g[0:6])
        tiles += [jnp.where(first_row, g[12:18], 0.0), pad, jnp.where(last_row, above, 0.0), pad]
        block = jnp.concatenate(tiles, axis=0).astype(BF16)
        for half in range(2):
            j = 2 * pair + half
            for group in range(GROUPS):
                at = half * C * ROWS + group * 128
                wt[group, :, 128 * j : 128 * j + 128] = block[:, at : at + 128]


def basis(x):
    base = (x * x) * (-4.0 * LOG2E)
    outer = base + (LIFT - 9.0 * LOG2E)
    slope = x * (12.0 * LOG2E)
    step = x * (4.0 * LOG2E)
    up = jnp.exp2(step - LOG2E)
    down = jnp.exp2(-LOG2E - step)
    left = jnp.exp2(outer - slope)
    middle = jnp.exp2(base + float(LIFT))
    right = jnp.exp2(outer + slope)
    half = x * (0.5 * 2.0**LIFT)
    silu = half + half * jnp.tanh(x * 0.5)
    return [left * down, left, left * up, middle * down, middle, middle * up, right * down, right, right * up, silu]


def bits(value, flips):
    return jnp.bitwise_xor(value, flips) if flips else value


def kernel(
    n_lon, n_lat,
    feat_hbm, coef_hbm, edge_hbm, head_hbm, land_hbm, shift_hbm,
    tend_ref, fields_ref, sums_ref,
    feat, coef_ref, edge_ref, head_ref, land_ref, shift_ref, wt, bases, acc,
    north, south, to_east, to_west, got, side, sums_a, sums_b,
    feat_sem, weight_sem, send, recv, send_sum, recv_sum,
):
    lon, lat = lax.axis_index("lon"), lax.axis_index("lat")
    top, bottom = lat == n_lat - 1, lat == 0
    east = jnp.where(lon == n_lon - 1, 0, lon + 1)
    west = jnp.where(lon == 0, n_lon - 1, lon - 1)
    up_lat = jnp.where(top, lat, lat + 1)
    up_lon = jnp.where(top, n_lon - 1 - lon, lon)
    up_east = jnp.where(top, n_lon - 1 - east, east)
    up_west = jnp.where(top, n_lon - 1 - west, west)
    down_lat = jnp.where(bottom, lat, lat - 1)
    east_self, west_self = top & (up_east == lon), top & (up_west == lon)
    east_other, west_other = jnp.logical_not(east_self), jnp.logical_not(west_self)
    has_south = jnp.logical_not(bottom)

    weights_in = [
        pltpu.make_async_copy(src, dst, weight_sem.at[k])
        for k, (src, dst) in enumerate(
            [(edge_hbm, edge_ref), (head_hbm, head_ref), (coef_hbm, coef_ref), (land_hbm, land_ref), (shift_hbm, shift_ref)]
        )
    ]

    def feat_in(k):
        part = pl.ds(k * GROUP, GROUP)
        return pltpu.make_async_copy(feat_hbm.at[part], feat.at[part], feat_sem.at[k])

    for copy in weights_in + [feat_in(k) for k in range(GROUPS)]:
        copy.start()

    half = n_lon // 2
    first_sum = [(bits(lon, 2 * (d % half)), bits(lat, d // half)) for d in range(n_lon)]
    first_here = lon // 2 + half * lax.rem(lat, 2)
    second_sum = [(bits(lon, d % 2), bits(lat, d - d % 2)) for d in range(n_lat)]
    second_here = lat - lax.rem(lat, 2) + lax.rem(lon, 2)

    barrier = pltpu.get_barrier_semaphore()

    def greet(at_lon, at_lat):
        pl.semaphore_signal(barrier, inc=1, device_id={"lon": at_lon, "lat": at_lat}, device_id_type=MESH)

    greet(east, lat)
    greet(west, lat)
    greet(up_lon, up_lat)
    pl.when(east_other)(lambda: greet(up_east, up_lat))
    pl.when(west_other)(lambda: greet(up_west, up_lat))

    @pl.when(has_south)
    def _():
        greet(lon, down_lat)
        greet(east, down_lat)
        greet(west, down_lat)

    for at in first_sum[1:] + second_sum[1:]:
        greet(*at)
    greetings = n_lon + n_lat + 6 - jnp.where(east_self, 1, 0) - jnp.where(west_self, 1, 0) - jnp.where(bottom, 3, 0)

    def remote(src, dst, send, recv, at_lon, at_lat):
        return pltpu.make_async_remote_copy(
            src_ref=src, dst_ref=dst, send_sem=send, recv_sem=recv,
            device_id={"lon": at_lon, "lat": at_lat}, device_id_type=MESH,
        )

    @pl.when(bottom)
    def _():
        got[0:3] = jnp.zeros((3, 16, WIDE), F32)

    for copy in weights_in:
        copy.wait()
    fold_weights(coef_ref, edge_ref, head_ref, wt, top)

    acc[...] = jnp.zeros(acc.shape, F32)

    def step(k, carry):
        group, level = k // L, lax.rem(k, L)
        pl.when(level == 0)(lambda: feat_in(group).wait())
        for at in range(0, GROUP, STRIP):
            x = feat[pl.ds(group * GROUP + at, STRIP), level].astype(F32).reshape(STRIP * ROWS, COLS)
            for j, value in enumerate(basis(x)):
                row = 128 * j + ROWS * at
                bases[row : row + ROWS * STRIP, :] = value.astype(BF16)
        acc[level, :, 0:COLS] += dot(wt[group], bases[...])
        return carry

    lax.fori_loop(0, GROUPS * L, step, 0)

    lane, low = iota((ROWS, 128), 1), iota((ROWS, 128), 1) < 64
    low2 = iota((16, 128), 1) < 64
    row = iota((ROWS, WIDE), 0)
    zero = jnp.zeros((ROWS, WIDE), F32)

    def joined(parts):
        return jnp.concatenate(parts, axis=1)

    def stacked(parts):
        return jnp.concatenate(parts, axis=0)

    def lanes(x, by):
        return pltpu.roll(x, by % WIDE, 1)

    def rows(x, by):
        return pltpu.roll(x, by % 16, 0)

    def placed(entries):
        out = zero
        for at, value in entries:
            out = jnp.where(row == at, value, out)
        return out

    j = lax.shift_right_logical(iota((1, 128 * J), 1), 7)
    off = jnp.abs(j - 4)
    still = jnp.where(off == 1, math.exp(-1.0), jnp.where(off == 3, math.exp(-9.0), math.exp(-10.0)))
    still = jnp.where(off == 0, 1.0, jnp.where(j == NB, 0.0, still))
    outside = jnp.zeros((8, 128 * J), F32)
    for group in range(GROUPS):
        outside = outside + wt[group, 48:64, :].astype(F32)[8:16]
    outside = jnp.where(bottom, jnp.sum(outside * still, axis=1, keepdims=True), 0.0)
    outside = outside[0:2] + outside[2:4] + outside[4:6]
    first_row = (iota((ROWS, WIDE), 0) == 0) & (iota((ROWS, WIDE), 1) < COLS)
    outside = stacked([jnp.where(first_row, outside[c : c + 1], 0.0) for c in range(2)])

    own, above, below = [], [], []
    for level in range(L):
        a = acc[level] * (2.0**-LIFT)
        own.append(a[16:32] + lanes(a[0:16], 1) + lanes(a[32:48], -1) + outside)
        outer = a[48:64]
        before, after = lanes(outer, 1), lanes(outer, -1)
        below.append(outer[2:4] + before[0:2] + after[4:6])
        above.append(outer[10:12] + before[8:10] + after[12:14])
    total, total_up, total_down = own[0] + own[1], above[0] + above[1], below[0] + below[1]
    share = [stacked([total[8 * c : 8 * c + 8], placed([(0, total_up[c : c + 1]), (7, total_down[c : c + 1])])]) for c in range(2)]
    upper = own[1]

    ocean = joined([land_ref[...].astype(F32), zero[:, 0:128]])
    shift = joined([shift_ref[...], zero[:, 0:128]])

    def both(r):
        return [total[r : r + 1], total[8 + r : 9 + r]]

    none = [zero[0:1]]
    edge_n = stacked(
        [total_up] + both(7) + both(6) + both(5) + [above[1], ocean[7:8], ocean[6:7], ocean[5:6], shift[7:8]] + none * 2
    )
    edge_s = stacked(
        [total_down] + both(0) + both(1) + none * 2 + [below[1], ocean[0:1], ocean[1:2]] + none + [shift[0:1]] + none * 2
    )
    edge_e = stacked(share + [upper, ocean, shift])

    def eastern(x):
        return jnp.where(iota((x.shape[0], 128), 1) < 64, x[:, COLS:], x[:, COLS - 128 : COLS])

    def western(x):
        return jnp.where(iota((x.shape[0], 128), 1) < 64, x[:, 0:128], x[:, COLS:])

    corner = pl.ds(WIDE, 128), pl.ds(WIDE + 128, 128)
    for edge, ref in ((edge_n, north), (edge_s, south)):
        ref[:, 0:WIDE] = edge
        ref[:, WIDE : WIDE + 128] = eastern(edge)
        ref[:, WIDE + 128 :] = western(edge)
    to_east[...] = eastern(edge_e)
    to_west[...] = western(edge_e)

    whole, part = pl.ds(0, WIDE), pl.ds(0, 128)
    upward = jnp.where(top, 3, 0)
    sends = [
        (east_other, remote(north.at[:, corner[0]], got.at[upward + 1, :, part], send.at[1], recv.at[upward + 1], up_east, up_lat)),
        (west_other, remote(north.at[:, corner[1]], got.at[upward + 2, :, part], send.at[2], recv.at[upward + 2], up_west, up_lat)),
        (has_south, remote(south.at[:, corner[0]], got.at[4, :, part], send.at[4], recv.at[4], east, down_lat)),
        (has_south, remote(south.at[:, corner[1]], got.at[5, :, part], send.at[5], recv.at[5], west, down_lat)),
        (None, remote(north.at[:, whole], got.at[upward], send.at[0], recv.at[upward], up_lon, up_lat)),
        (has_south, remote(south.at[:, whole], got.at[3], send.at[3], recv.at[3], lon, down_lat)),
        (None, remote(to_east, side.at[0], send.at[6], recv.at[6], east, lat)),
        (None, remote(to_west, side.at[1], send.at[7], recv.at[7], west, lat)),
    ]

    def arrival(src, dst, k):
        return remote(src, dst, send.at[0], recv.at[k], east, lat)

    corner_n = north.at[:, corner[0]]
    arrivals = [
        (None, arrival(to_east, side.at[0], 6)),
        (None, arrival(to_west, side.at[1], 7)),
        (has_south, arrival(north.at[:, whole], got.at[0], 0)),
        (has_south, arrival(corner_n, got.at[1, :, part], 1)),
        (has_south, arrival(corner_n, got.at[2, :, part], 2)),
        (None, arrival(north.at[:, whole], got.at[3], 3)),
        (east_other, arrival(corner_n, got.at[4, :, part], 4)),
        (west_other, arrival(corner_n, got.at[5, :, part], 5)),
    ]

    def each(entries, act):
        for cond, copy in entries:
            if cond is None:
                act(copy)
            else:
                pl.when(cond)(functools.partial(act, copy))

    pl.semaphore_wait(barrier, greetings)
    each(sends, lambda copy: copy.start())

    @pl.when(east_self)
    def _():
        got[4, :, 0:128] = north[:, WIDE : WIDE + 128]

    @pl.when(west_self)
    def _():
        got[5, :, 0:128] = north[:, WIDE + 128 :]

    each(arrivals, lambda copy: copy.wait_recv())

    def arrived(k):
        parts = [got[k, :, 128 * t : 128 * t + 128] for t in range(5)]
        w, e = got[k + 1, :, 0:128], got[k + 2, :, 0:128]
        return [
            parts[0] + jnp.where(low2, w, 0.0), parts[1], parts[2],
            parts[3] + jnp.where(low2, 0.0, e), parts[4] + jnp.where(low2, e, w),
        ]

    backwards = 127 - lane

    def turned(x):
        return stacked([jnp.take_along_axis(x[r : r + 8], backwards, axis=1) for r in (0, 8)])

    s_rows = joined(arrived(0))
    n_parts = arrived(3)
    flipped = [turned(x) for x in n_parts]
    flipped = flipped[3::-1] + flipped[4:]
    n_rows = joined([jnp.where(top, f, n) for f, n in zip(flipped, n_parts)])
    from_west, from_east = side[0], side[1]

    def with_sides(x, at):
        count = x.shape[0]
        w, e = from_west[at : at + count], from_east[at : at + count]
        near = iota((count, 128), 1) < 64
        return joined([
            x[:, 0:128] + jnp.where(near, w, 0.0),
            x[:, 128 : COLS - 128],
            x[:, COLS - 128 : COLS] + jnp.where(near, 0.0, e),
            x[:, COLS:] + jnp.where(near, e, w),
        ])

    def one(x, k):
        return x[k : k + 1]

    m = stacked([
        with_sides(ocean, 48),
        placed([(r, one(n_rows, 10 + r)) for r in range(3)] + [(7 - r, one(s_rows, 10 + r)) for r in range(3)]),
    ])
    s = stacked([with_sides(shift, 56), placed([(0, one(n_rows, 13)), (7, one(s_rows, 13))])])
    eastward, northward = [
        m * (
            with_sides(share[c], 16 * c)
            + stacked([
                placed([(0, one(s_rows, c)), (7, one(n_rows, c))]),
                placed([(r, one(n_rows, 2 + 2 * r + c)) for r in range(3)] + [(7 - r, one(s_rows, 2 + 2 * r + c)) for r in range(3)]),
            ])
        )
        for c in range(2)
    ]
    r = m * (eastward - lanes(eastward, 1) + northward - rows(northward, 1))
    beyond = m * (eastward - lanes(eastward, -1) + northward - rows(northward, -1))
    r = stacked([r[0:8], jnp.where(top & (row < 2), beyond[8:16], r[8:16])])

    def operate(v):
        return m * ((4.0 + s) * v - (lanes(v, 1) + lanes(v, -1) + rows(v, 1) + rows(v, -1)))

    q1 = operate(r)
    q2 = operate(q1)[0:8, 0:COLS]
    r, q1 = r[0:8, 0:COLS], q1[0:8, 0:COLS]

    def summed(x):
        x = x[:, 0:128] + x[:, 128:256] + x[:, 256:384] + x[:, 384:512]
        return jnp.sum(x, axis=0, keepdims=True)

    dots = [summed(r * r), summed(r * q1), summed(q1 * q1), summed(r * q2), summed(q1 * q2)]

    def spread(value, ref, stage, here, devices):
        ref[here] = value
        copies = [remote(ref.at[here], ref.at[here], send_sum.at[stage], recv_sum.at[stage], *at) for at in devices[1:]]
        for copy in copies:
            copy.start()

    def collect(ref, stage, count):
        several = ref.at[pl.ds(0, count - 1)]
        copy = remote(several, several, send_sum.at[stage], recv_sum.at[stage], east, lat)
        copy.wait_recv()
        copy.wait_send()
        return jnp.sum(ref[...], axis=0)

    spread(stacked(dots + [jnp.zeros((3, 128), F32)]), sums_a, 0, first_here, first_sum)

    ocean = ocean[:, 0:COLS]
    upper = with_sides(upper, 32)
    for c in range(2):
        one_level = upper[8 * c : 8 * c + 8] + placed([(0, one(s_rows, 8 + c)), (7, one(n_rows, 8 + c))])
        one_level = ocean * one_level[:, 0:COLS]
        whole = (eastward, northward)[c][0:8, 0:COLS]
        tend_ref[c, 0] = (whole - one_level).astype(BF16)
        tend_ref[c, 1] = one_level.astype(BF16)
    for k, value in enumerate((r, q1, q2)):
        fields_ref[8 * k : 8 * k + 8, :] = value
    each(sends, lambda copy: copy.wait_send())

    spread(collect(sums_a, 0, n_lon), sums_b, 1, second_here, second_sum)
    sums_ref[...] = collect(sums_b, 1, n_lat)


def finish(fields_ref, sums_ref, tend_in, tend_ref, surf_ref, res_ref):
    r, q1, q2 = fields_ref[0:8, :], fields_ref[8:16, :], fields_ref[16:24, :]
    value = jnp.sum(sums_ref[...], axis=1, keepdims=True)
    rr, rq, qq, rq2, qq2 = [value[k : k + 1] for k in range(5)]
    a1 = rr / rq
    new = rr - 2.0 * a1 * rq + a1 * a1 * qq
    lead = 1.0 + new / rr
    a2 = new / (lead * lead * rq - lead * a1 * (rq2 + qq) + a1 * a1 * qq2)
    surf_ref[...] = a1 * r + a2 * (lead * r - a1 * q1)
    res_ref[...] = r - a1 * q1 - a2 * (lead * q1 - a1 * q2)
    tend_ref[...] = tend_in[...]


def body(features, spline_coef, edge_mask, head_weight, land_mask, shift_coef):
    n_lon, n_lat = lax.axis_size("lon"), lax.axis_size("lat")
    vmem = pl.BlockSpec(memory_space=pltpu.VMEM)
    dma = pltpu.SemaphoreType.DMA
    tend_shape = jax.ShapeDtypeStruct((2, L, ROWS, COLS), BF16)
    field_shape = jax.ShapeDtypeStruct((ROWS, COLS), F32)
    scratch = [
        pltpu.VMEM((C, L, ROWS, COLS), BF16),
        pltpu.VMEM((9 * C, C * J), BF16),
        pltpu.VMEM((C, C), jnp.int32),
        pltpu.VMEM((2, C), BF16),
        pltpu.VMEM((ROWS, COLS), jnp.int32),
        pltpu.VMEM((ROWS, COLS), F32),
        pltpu.VMEM((GROUPS, 64, 128 * J), BF16),
        pltpu.VMEM((128 * J, COLS), BF16),
        pltpu.VMEM((L, 64, WIDE), F32),
        pltpu.VMEM((16, WIDE + 256), F32),
        pltpu.VMEM((16, WIDE + 256), F32),
        pltpu.VMEM((64, 128), F32),
        pltpu.VMEM((64, 128), F32),
        pltpu.VMEM((6, 16, WIDE), F32),
        pltpu.VMEM((2, 64, 128), F32),
        pltpu.VMEM((n_lon, 8, 128), F32),
        pltpu.VMEM((n_lat, 8, 128), F32),
        dma((GROUPS,)), dma((5,)), dma((8,)), dma((8,)), dma((2,)), dma((2,)),
    ]
    tendency, fields, sums = pl.pallas_call(
        functools.partial(kernel, n_lon, n_lat),
        out_shape=(
            tend_shape,
            jax.ShapeDtypeStruct((3 * ROWS, COLS), F32),
            jax.ShapeDtypeStruct((8, 128), F32),
        ),
        in_specs=[pl.BlockSpec(memory_space=pl.ANY)] * 6,
        out_specs=(vmem, vmem, vmem),
        scratch_shapes=scratch,
        compiler_params=pltpu.CompilerParams(collective_id=0, has_side_effects=True),
        name="closure_and_sums",
    )(features, spline_coef, edge_mask, head_weight, land_mask, shift_coef)
    return pl.pallas_call(
        finish,
        out_shape=(tend_shape, field_shape, field_shape),
        in_specs=[vmem] * 3,
        out_specs=(vmem, vmem, vmem),
        name="finish",
    )(fields, sums, tendency)


def solution(mesh):
    in_specs = (P(None, None, "lat", "lon"), P(), P(), P(), P("lat", "lon"), P("lat", "lon"))
    out_specs = (P(None, None, "lat", "lon"), P("lat", "lon"), P("lat", "lon"))
    return jax.shard_map(body, mesh=mesh, in_specs=in_specs, out_specs=out_specs, check_vma=False)
```

time: 37.9 us -> 31.1 us (0.82)
  local copies, waits for them, and re-layouts: 6.79 us -> 0 us
    unnamed x15 -> x0, local copies, waits for them, and re-layouts: 6.79 us -> none
    pallas_call x1 -> x2, Pallas kernels: 30.2 us -> 30.3 us  [the longest x1 28.8 us: body(): pl.pallas_call(functools.partial(kernel, n_lon, n_lat), out_shape=(tend_s...]
where the time goes in v2:
time: 31.1 us; the launch traced here: 31 us
  Pallas kernels  30.3 us (97%)
  between operations  0.64 us (2%)
    pallas_call x1, Pallas kernels, body(): pl.pallas_call(functools.partial(kernel, n_lon, n_lat), out_shape=(tend_s...  28.8 us
    pallas_call x1, Pallas kernels, body(): pl.pallas_call(finish, out_shape=(tend_shape, field_shape, field_shape),...  1.55 us

profile of v2, /device:TPU:1, one launch (start us, length us, event | category | flops | bytes accessed | tf_op | source)
XLA Modules:
  0.0 31.0 jit_solution(1516526196428839729)
XLA Ops:
  0.6 28.8 %closure_and_sums.1 = (bf16[2,2,8,512]{3,2,1,0:T(8,128)(2,1)}, f32[24,512]{1,0:T(8,128)}, f32[8,128]{1,0:T(8,128)}) custom-call(bf16[48,2,8,512]{3,2,1,0:T(8,128)(2,1)} %feat_hbm.1, bf16[432,480]{1,0:T(8,128)(2,1)} %coef_hbm.1, s32[48,48]{1,0:T(8,128)} %edge_hbm.1, bf16[2,48]{1,0:T(2,128)(2,1)} %head_hbm.1, s32[8,512]{1,0:T(8,128)} %land_hbm.1, ...), custom_call_target="tpu_custom_call" | custom-call | tf_op jit(solution)/shard_map/closure_and_sums/pallas_call | solution.py:457
  29.4 1.6 %finish.1 = (bf16[2,2,8,512]{3,2,1,0:T(8,128)(2,1)}, f32[8,512]{1,0:T(8,128)}, f32[8,512]{1,0:T(8,128)}) custom-call(f32[24,512]{1,0:T(8,128)} %get-tuple-element.6.fields_ref, f32[8,128]{1,0:T(8,128)} %get-tuple-element.7.sums_ref, bf16[2,2,8,512]{3,2,1,0:T(8,128)(2,1)} %get-tuple-element.8.tend_in), custom_call_target="tpu_custom_call" | custom-call | tf_op jit(solution)/shard_map/finish/pallas_call | solution.py:470

commit v3 on v2

--- a/solution.py
+++ b/solution.py
@@ -390,14 +390,17 @@
         for copy in copies:
             copy.start()
 
+    def all_copies(ref, stage, count):
+        several = ref.at[pl.ds(0, count - 1)]
+        return remote(several, several, send_sum.at[stage], recv_sum.at[stage], east, lat)
+
     def collect(ref, stage, count):
-        several = ref.at[pl.ds(0, count - 1)]
-        copy = remote(several, several, send_sum.at[stage], recv_sum.at[stage], east, lat)
-        copy.wait_recv()
-        copy.wait_send()
+        all_copies(ref, stage, count).wait_recv()
         return jnp.sum(ref[...], axis=0)
 
-    spread(stacked(dots + [jnp.zeros((3, 128), F32)]), sums_a, 0, first_here, first_sum)
+    dots = jnp.sum(stacked(dots + [jnp.zeros((3, 128), F32)]), axis=1, keepdims=True)
+    dots = jnp.sum(jnp.where(lane == iota((ROWS, 128), 0), dots, 0.0), axis=0, keepdims=True)
+    spread(dots, sums_a, 0, first_here, first_sum)
 
     ocean = ocean[:, 0:COLS]
     upper = with_sides(upper, 32)
@@ -413,12 +416,13 @@
 
     spread(collect(sums_a, 0, n_lon), sums_b, 1, second_here, second_sum)
     sums_ref[...] = collect(sums_b, 1, n_lat)
+    all_copies(sums_a, 0, n_lon).wait_send()
+    all_copies(sums_b, 1, n_lat).wait_send()
 
 
 def finish(fields_ref, sums_ref, tend_in, tend_ref, surf_ref, res_ref):
     r, q1, q2 = fields_ref[0:8, :], fields_ref[8:16, :], fields_ref[16:24, :]
-    value = jnp.sum(sums_ref[...], axis=1, keepdims=True)
-    rr, rq, qq, rq2, qq2 = [value[k : k + 1] for k in range(5)]
+    rr, rq, qq, rq2, qq2 = [sums_ref[0:1, k : k + 1] for k in range(5)]
     a1 = rr / rq
     new = rr - 2.0 * a1 * rq + a1 * a1 * qq
     lead = 1.0 + new / rr
@@ -450,16 +454,16 @@
         pltpu.VMEM((64, 128), F32),
         pltpu.VMEM((6, 16, WIDE), F32),
         pltpu.VMEM((2, 64, 128), F32),
-        pltpu.VMEM((n_lon, 8, 128), F32),
-        pltpu.VMEM((n_lat, 8, 128), F32),
+        pltpu.VMEM((n_lon, 1, 128), F32),
+        pltpu.VMEM((n_lat, 1, 128), F32),
         dma((GROUPS,)), dma((5,)), dma((8,)), dma((8,)), dma((2,)), dma((2,)),
     ]
     tendency, fields, sums = pl.pallas_call(
         functools.partial(kernel, n_lon, n_lat),
         out_shape=(
-            tend_shape,
-            jax.ShapeDtypeStruct((3 * ROWS, COLS), F32),
-            jax.ShapeDtypeStruct((8, 128), F32),
+            pltpu.VMEM((2, L, ROWS, COLS), BF16),
+            pltpu.VMEM((3 * ROWS, COLS), F32),
+            pltpu.VMEM((1, 128), F32),
         ),
         in_specs=[pl.BlockSpec(memory_space=pl.ANY)] * 6,
         out_specs=(vmem, vmem, vmem),
@@ -472,6 +476,7 @@
         out_shape=(tend_shape, field_shape, field_shape),
         in_specs=[vmem] * 3,
         out_specs=(vmem, vmem, vmem),
+        compiler_params=pltpu.CompilerParams(vmem_limit_bytes=4 * 1024 * 1024),
         name="finish",
     )(fields, sums, tendency)
 

time: 31.1 us -> 29 us (0.932)
  Pallas kernels: 30.3 us -> 28.2 us
    pallas_call x1, Pallas kernels: 28.8 us -> 27.4 us  [body(): pl.pallas_call(functools.partial(kernel, n_lon, n_lat), out_shape=(pltpu....]
    pallas_call x1, Pallas kernels: 1.55 us -> 0.83 us  [body(): pl.pallas_call(finish, out_shape=(tend_shape, field_shape, field_shape),...]
where the time goes in v3:
time: 29 us; the launch traced here: 28.9 us
  Pallas kernels  28.2 us (97%)
  between operations  0.64 us (2%)
    pallas_call x1, Pallas kernels, body(): pl.pallas_call(functools.partial(kernel, n_lon, n_lat), out_shape=(pltpu....  27.4 us
    pallas_call x1, Pallas kernels, body(): pl.pallas_call(finish, out_shape=(tend_shape, field_shape, field_shape),...  0.83 us

profile of v3, /device:TPU:1, one launch (start us, length us, event | category | flops | bytes accessed | tf_op | source)
XLA Modules:
  0.0 28.9 jit_solution(7892355929071493082)
XLA Ops:
  0.6 27.4 %closure_and_sums.1 = (bf16[2,2,8,512]{3,2,1,0:T(8,128)(2,1)S(1)}, f32[24,512]{1,0:T(8,128)S(1)}, f32[1,128]{1,0:T(1,128)S(1)}) custom-call(bf16[48,2,8,512]{3,2,1,0:T(8,128)(2,1)} %feat_hbm.1, bf16[432,480]{1,0:T(8,128)(2,1)} %coef_hbm.1, s32[48,48]{1,0:T(8,128)} %edge_hbm.1, bf16[2,48]{1,0:T(2,128)(2,1)} %head_hbm.1, s32[8,512]{1,0:T(8,128)} %land_hbm.1, ...), custom_call_target="tpu_custom_call" | custom-call | tf_op jit(solution)/shard_map/closure_and_sums/pallas_call | solution.py:461
  28.0 0.8 %finish.1 = (bf16[2,2,8,512]{3,2,1,0:T(8,128)(2,1)}, f32[8,512]{1,0:T(8,128)}, f32[8,512]{1,0:T(8,128)}) custom-call(f32[24,512]{1,0:T(8,128)S(1)} %get-tuple-element.6.fields_ref, f32[1,128]{1,0:T(1,128)S(1)} %get-tuple-element.7.sums_ref, bf16[2,2,8,512]{3,2,1,0:T(8,128)(2,1)S(1)} %get-tuple-element.8.tend_in), custom_call_target="tpu_custom_call" | custom-call | tf_op jit(solution)/shard_map/finish/pallas_call | solution.py:474

commit v4 on v3

--- a/solution.py
+++ b/solution.py
@@ -19,7 +19,7 @@
 BF16 = jnp.bfloat16
 MESH = pl.DeviceIdType.MESH
 LOG2E = math.log2(math.e)
-LIFT = 29
+LIFT = 82
 GROUP = 16
 GROUPS = C // GROUP
 STRIP = 2
@@ -53,7 +53,8 @@
     folded = dot(head, jnp.concatenate(masked, axis=0))
     lane = iota((1, C * J), 1)
     j = lane - J * lax.shift_right_logical(lane * 6554, 16)
-    scale = jnp.where((j == 0) | (j == 8), math.exp(-6.0), jnp.where((j == 2) | (j == 6), math.exp(6.0), 1.0))
+    off = jnp.abs(j - NB // 2).astype(F32)
+    scale = jnp.where(j == NB, 2.0**LIFT, jnp.exp(-off * off))
     folded = (folded * scale).astype(BF16)
     q = iota((1, 64 * J), 1)
     source = jnp.where((q & 63) < C, (q & 63) * J + lax.shift_right_logical(q, 6), -1)
@@ -85,18 +86,16 @@
 
 
 def basis(x):
-    base = (x * x) * (-4.0 * LOG2E)
-    outer = base + (LIFT - 9.0 * LOG2E)
-    slope = x * (12.0 * LOG2E)
-    step = x * (4.0 * LOG2E)
-    up = jnp.exp2(step - LOG2E)
-    down = jnp.exp2(-LOG2E - step)
-    left = jnp.exp2(outer - slope)
-    middle = jnp.exp2(base + float(LIFT))
-    right = jnp.exp2(outer + slope)
-    half = x * (0.5 * 2.0**LIFT)
-    silu = half + half * jnp.tanh(x * 0.5)
-    return [left * down, left, left * up, middle * down, middle, middle * up, right * down, right, right * up, silu]
+    half = x * 0.5
+    middle = jnp.exp2((half * half) * (-16.0 * LOG2E) + float(LIFT))
+    up = jnp.exp2(half * (8.0 * LOG2E))
+    down = jnp.exp2(half * (-8.0 * LOG2E))
+    silu = half + half * jnp.tanh(half)
+    left, right = [middle], [middle]
+    for _ in range(NB // 2):
+        left.append(left[-1] * down)
+        right.append(right[-1] * up)
+    return left[:0:-1] + right + [silu]
 
 
 def bits(value, flips):
@@ -139,10 +138,10 @@
         copy.start()
 
     half = n_lon // 2
-    first_sum = [(bits(lon, 2 * (d % half)), bits(lat, d // half)) for d in range(n_lon)]
-    first_here = lon // 2 + half * lax.rem(lat, 2)
-    second_sum = [(bits(lon, d % 2), bits(lat, d - d % 2)) for d in range(n_lat)]
-    second_here = lat - lax.rem(lat, 2) + lax.rem(lon, 2)
+    first_sum = [(bits(lon, d % 2), bits(lat, d - d % 2)) for d in range(n_lat)]
+    first_here = lat - lax.rem(lat, 2) + lax.rem(lon, 2)
+    second_sum = [(bits(lon, 2 * (d % half)), bits(lat, d // half)) for d in range(n_lon)]
+    second_here = lon // 2 + half * lax.rem(lat, 2)
 
     barrier = pltpu.get_barrier_semaphore()
 
@@ -218,9 +217,7 @@
         return out
 
     j = lax.shift_right_logical(iota((1, 128 * J), 1), 7)
-    off = jnp.abs(j - 4)
-    still = jnp.where(off == 1, math.exp(-1.0), jnp.where(off == 3, math.exp(-9.0), math.exp(-10.0)))
-    still = jnp.where(off == 0, 1.0, jnp.where(j == NB, 0.0, still))
+    still = jnp.where(j == NB, 0.0, 1.0)
     outside = jnp.zeros((8, 128 * J), F32)
     for group in range(GROUPS):
         outside = outside + wt[group, 48:64, :].astype(F32)[8:16]
@@ -414,10 +411,10 @@
         fields_ref[8 * k : 8 * k + 8, :] = value
     each(sends, lambda copy: copy.wait_send())
 
-    spread(collect(sums_a, 0, n_lon), sums_b, 1, second_here, second_sum)
-    sums_ref[...] = collect(sums_b, 1, n_lat)
-    all_copies(sums_a, 0, n_lon).wait_send()
-    all_copies(sums_b, 1, n_lat).wait_send()
+    spread(collect(sums_a, 0, n_lat), sums_b, 1, second_here, second_sum)
+    sums_ref[...] = collect(sums_b, 1, n_lon)
+    all_copies(sums_a, 0, n_lat).wait_send()
+    all_copies(sums_b, 1, n_lon).wait_send()
 
 
 def finish(fields_ref, sums_ref, tend_in, tend_ref, surf_ref, res_ref):
@@ -454,8 +451,8 @@
         pltpu.VMEM((64, 128), F32),
         pltpu.VMEM((6, 16, WIDE), F32),
         pltpu.VMEM((2, 64, 128), F32),
+        pltpu.VMEM((n_lat, 1, 128), F32),
         pltpu.VMEM((n_lon, 1, 128), F32),
-        pltpu.VMEM((n_lat, 1, 128), F32),
         dma((GROUPS,)), dma((5,)), dma((8,)), dma((8,)), dma((2,)), dma((2,)),
     ]
     tendency, fields, sums = pl.pallas_call(

time: 29 us -> 27.7 us (0.955)
  Pallas kernels: 28.2 us -> 27 us
    pallas_call x1, Pallas kernels: 27.4 us -> 26.1 us  [body(): pl.pallas_call(functools.partial(kernel, n_lon, n_lat), out_shape=(pltpu....]
where the time goes in v4:
time: 27.7 us; the launch traced here: 27.6 us
  Pallas kernels  27 us (97%)
  between operations  0.64 us (2%)
    pallas_call x1, Pallas kernels, body(): pl.pallas_call(functools.partial(kernel, n_lon, n_lat), out_shape=(pltpu....  26.1 us
    pallas_call x1, Pallas kernels, body(): pl.pallas_call(finish, out_shape=(tend_shape, field_shape, field_shape),...  0.83 us

profile of v4, /device:TPU:1, one launch (start us, length us, event | category | flops | bytes accessed | tf_op | source)
XLA Modules:
  0.0 27.6 jit_solution(7695123028964450105)
XLA Ops:
  0.6 26.1 %closure_and_sums.1 = (bf16[2,2,8,512]{3,2,1,0:T(8,128)(2,1)S(1)}, f32[24,512]{1,0:T(8,128)S(1)}, f32[1,128]{1,0:T(1,128)S(1)}) custom-call(bf16[48,2,8,512]{3,2,1,0:T(8,128)(2,1)} %feat_hbm.1, bf16[432,480]{1,0:T(8,128)(2,1)} %coef_hbm.1, s32[48,48]{1,0:T(8,128)} %edge_hbm.1, bf16[2,48]{1,0:T(2,128)(2,1)} %head_hbm.1, s32[8,512]{1,0:T(8,128)} %land_hbm.1, ...), custom_call_target="tpu_custom_call" | custom-call | tf_op jit(solution)/shard_map/closure_and_sums/pallas_call | solution.py:458
  26.8 0.8 %finish.1 = (bf16[2,2,8,512]{3,2,1,0:T(8,128)(2,1)}, f32[8,512]{1,0:T(8,128)}, f32[8,512]{1,0:T(8,128)}) custom-call(f32[24,512]{1,0:T(8,128)S(1)} %get-tuple-element.6.fields_ref, f32[1,128]{1,0:T(1,128)S(1)} %get-tuple-element.7.sums_ref, bf16[2,2,8,512]{3,2,1,0:T(8,128)(2,1)S(1)} %get-tuple-element.8.tend_in), custom_call_target="tpu_custom_call" | custom-call | tf_op jit(solution)/shard_map/finish/pallas_call | solution.py:471

commit v5 on v4

--- a/solution.py
+++ b/solution.py
@@ -22,7 +22,7 @@
 LIFT = 82
 GROUP = 16
 GROUPS = C // GROUP
-STRIP = 2
+CHUNK = GROUP * ROWS * J
 
 
 def iota(shape, axis):
@@ -48,27 +48,23 @@
     offset = lax.shift_right_logical(q * 1366, 16)
     head = jnp.where((r & 1) == 0, head[0:1], head[1:2])
     head = jnp.where(lax.shift_right_logical(r, 1) == offset, head, 0.0).astype(BF16)
-    folded = jnp.zeros((24, C * J), F32)
     masked = [coef_ref[C * k : C * k + C, :] * keep for k in range(9)]
     folded = dot(head, jnp.concatenate(masked, axis=0))
     lane = iota((1, C * J), 1)
     j = lane - J * lax.shift_right_logical(lane * 6554, 16)
     off = jnp.abs(j - NB // 2).astype(F32)
     scale = jnp.where(j == NB, 2.0**LIFT, jnp.exp(-off * off))
-    folded = (folded * scale).astype(BF16)
-    q = iota((1, 64 * J), 1)
-    source = jnp.where((q & 63) < C, (q & 63) * J + lax.shift_right_logical(q, 6), -1)
-    folded = dot(folded, ones_where(iota((C * J, 64 * J), 0) == source)).astype(BF16)
-    q = iota((1, 2 * C * ROWS), 1)
-    second = jnp.where(q >= C * ROWS, 1, 0)
-    source = second * 64 + lax.shift_right_logical(q - second * (C * ROWS), 3)
-    expand = ones_where(iota((128, 2 * C * ROWS), 0) == source)
-    y_out = iota((ROWS, 2 * C * ROWS), 0)
-    y_in = iota((ROWS, 2 * C * ROWS), 1) & 7
+    folded = folded * scale
+    q = iota((1, CHUNK), 1)
+    strip = lax.shift_right_logical(q * 13108, 21)
+    source = (2 * strip + (lax.shift_right_logical(q, 3) & 1)) * J + lax.shift_right_logical(q - strip * (2 * ROWS * J), 4)
+    expand = ones_where(iota((GROUP * J, CHUNK), 0) == source)
+    y_out = iota((ROWS, CHUNK), 0)
+    y_in = iota((ROWS, CHUNK), 1) & 7
     first_row, last_row = y_in[0:6] == 0, y_in[0:6] == 7
-    pad = jnp.zeros((2, 2 * C * ROWS), F32)
-    for pair in range(J // 2):
-        g = dot(folded[:, 128 * pair : 128 * pair + 128], expand)
+    pad = jnp.zeros((2, CHUNK), F32)
+    for group in range(GROUPS):
+        g = dot(folded[:, GROUP * J * group : GROUP * J * (group + 1)].astype(BF16), expand)
         tiles = []
         for k in range(6):
             tile = jnp.where(y_in == y_out - 1, g[k : k + 1], 0.0)
@@ -77,12 +73,7 @@
         mirrored = jnp.concatenate([g[16:18], g[14:16], g[12:14]], axis=0)
         above = jnp.where(top, mirrored, g[0:6])
         tiles += [jnp.where(first_row, g[12:18], 0.0), pad, jnp.where(last_row, above, 0.0), pad]
-        block = jnp.concatenate(tiles, axis=0).astype(BF16)
-        for half in range(2):
-            j = 2 * pair + half
-            for group in range(GROUPS):
-                at = half * C * ROWS + group * 128
-                wt[group, :, 128 * j : 128 * j + 128] = block[:, at : at + 128]
+        wt[group] = jnp.concatenate(tiles, axis=0).astype(BF16)
 
 
 def basis(x):
@@ -106,7 +97,7 @@
     n_lon, n_lat,
     feat_hbm, coef_hbm, edge_hbm, head_hbm, land_hbm, shift_hbm,
     tend_ref, fields_ref, sums_ref,
-    feat, coef_ref, edge_ref, head_ref, land_ref, shift_ref, wt, bases, acc,
+    feat, coef_ref, edge_ref, head_ref, land_ref, shift_ref, wt, bases_a, bases_b, acc,
     north, south, to_east, to_west, got, side, sums_a, sums_b,
     feat_sem, weight_sem, send, recv, send_sum, recv_sum,
 ):
@@ -138,9 +129,16 @@
         copy.start()
 
     half = n_lon // 2
-    first_sum = [(bits(lon, d % 2), bits(lat, d - d % 2)) for d in range(n_lat)]
+    ring = {0: 0, 1: 1, 2: 2, 3: 3, 4: 4, 5: 3, 6: 2, 7: 2}
+
+    def far_first(count, hops):
+        return sorted(range(1, count), key=lambda d: -hops(d))
+
+    first_order = far_first(n_lat, lambda d: ring.get(d // 2, 0))
+    first_sum = [(bits(lon, d % 2), bits(lat, d - d % 2)) for d in first_order]
     first_here = lat - lax.rem(lat, 2) + lax.rem(lon, 2)
-    second_sum = [(bits(lon, 2 * (d % half)), bits(lat, d // half)) for d in range(n_lon)]
+    second_order = far_first(n_lon, lambda d: (0, 1, 2, 1)[d % 4] + (0, 2, 1, 1)[d // 4 % 4])
+    second_sum = [(bits(lon, 2 * (d % half)), bits(lat, d // half)) for d in second_order]
     second_here = lon // 2 + half * lax.rem(lat, 2)
 
     barrier = pltpu.get_barrier_semaphore()
@@ -160,7 +158,7 @@
         greet(east, down_lat)
         greet(west, down_lat)
 
-    for at in first_sum[1:] + second_sum[1:]:
+    for at in first_sum + second_sum:
         greet(*at)
     greetings = n_lon + n_lat + 6 - jnp.where(east_self, 1, 0) - jnp.where(west_self, 1, 0) - jnp.where(bottom, 3, 0)
 
@@ -176,22 +174,45 @@
 
     for copy in weights_in:
         copy.wait()
+    feat_in(0).wait()
     fold_weights(coef_ref, edge_ref, head_ref, wt, top)
 
     acc[...] = jnp.zeros(acc.shape, F32)
 
-    def step(k, carry):
-        group, level = k // L, lax.rem(k, L)
-        pl.when(level == 0)(lambda: feat_in(group).wait())
-        for at in range(0, GROUP, STRIP):
-            x = feat[pl.ds(group * GROUP + at, STRIP), level].astype(F32).reshape(STRIP * ROWS, COLS)
+    def expanded(k, out):
+        for at in range(0, GROUP, 2):
+            x = feat[pl.ds((k // L) * GROUP + at, 2), lax.rem(k, L)].astype(F32).reshape(2 * ROWS, COLS)
             for j, value in enumerate(basis(x)):
-                row = 128 * j + ROWS * at
-                bases[row : row + ROWS * STRIP, :] = value.astype(BF16)
-        acc[level, :, 0:COLS] += dot(wt[group], bases[...])
+                row = (at * J + 2 * j) * ROWS
+                out[row : row + 2 * ROWS, :] = value.astype(BF16)
+
+    def contracted(k, bases):
+        acc[lax.rem(k, L), :, 0:COLS] += dot(wt[k // L], bases[...])
+
+    expanded(0, bases_a)
+    for k in range(1, GROUPS):
+        feat_in(k).wait()
+
+    def step(i, carry):
+        expanded(2 * i + 1, bases_b)
+        contracted(2 * i, bases_a)
+        expanded(jnp.minimum(2 * i + 2, L * GROUPS - 1), bases_a)
+        contracted(2 * i + 1, bases_b)
         return carry
 
-    lax.fori_loop(0, GROUPS * L, step, 0)
+    lax.fori_loop(0, GROUPS * L // 2, step, 0)
+
+    @pl.when(bottom)
+    def _():
+        q = iota((1, CHUNK), 1)
+        j = lax.shift_right_logical(q - lax.shift_right_logical(q * 13108, 21) * (2 * ROWS * J), 4)
+        outside = jnp.zeros((8, CHUNK), F32)
+        for group in range(GROUPS):
+            outside = outside + wt[group, 48:64, :].astype(F32)[8:16]
+        outside = jnp.sum(jnp.where(j < NB, outside, 0.0), axis=1, keepdims=True) * (2.0**LIFT)
+        for level in range(L):
+            for c in range(2):
+                acc[level, 16 + 8 * c : 17 + 8 * c, 0:COLS] += outside[c : c + 1] + outside[c + 2 : c + 3] + outside[c + 4 : c + 5]
 
     lane, low = iota((ROWS, 128), 1), iota((ROWS, 128), 1) < 64
     low2 = iota((16, 128), 1) < 64
@@ -216,20 +237,10 @@
             out = jnp.where(row == at, value, out)
         return out
 
-    j = lax.shift_right_logical(iota((1, 128 * J), 1), 7)
-    still = jnp.where(j == NB, 0.0, 1.0)
-    outside = jnp.zeros((8, 128 * J), F32)
-    for group in range(GROUPS):
-        outside = outside + wt[group, 48:64, :].astype(F32)[8:16]
-    outside = jnp.where(bottom, jnp.sum(outside * still, axis=1, keepdims=True), 0.0)
-    outside = outside[0:2] + outside[2:4] + outside[4:6]
-    first_row = (iota((ROWS, WIDE), 0) == 0) & (iota((ROWS, WIDE), 1) < COLS)
-    outside = stacked([jnp.where(first_row, outside[c : c + 1], 0.0) for c in range(2)])
-
     own, above, below = [], [], []
     for level in range(L):
         a = acc[level] * (2.0**-LIFT)
-        own.append(a[16:32] + lanes(a[0:16], 1) + lanes(a[32:48], -1) + outside)
+        own.append(a[16:32] + lanes(a[0:16], 1) + lanes(a[32:48], -1))
         outer = a[48:64]
         before, after = lanes(outer, 1), lanes(outer, -1)
         below.append(outer[2:4] + before[0:2] + after[4:6])
@@ -383,7 +394,7 @@
 
     def spread(value, ref, stage, here, devices):
         ref[here] = value
-        copies = [remote(ref.at[here], ref.at[here], send_sum.at[stage], recv_sum.at[stage], *at) for at in devices[1:]]
+        copies = [remote(ref.at[here], ref.at[here], send_sum.at[stage], recv_sum.at[stage], *at) for at in devices]
         for copy in copies:
             copy.start()
 
@@ -442,8 +453,9 @@
         pltpu.VMEM((2, C), BF16),
         pltpu.VMEM((ROWS, COLS), jnp.int32),
         pltpu.VMEM((ROWS, COLS), F32),
-        pltpu.VMEM((GROUPS, 64, 128 * J), BF16),
-        pltpu.VMEM((128 * J, COLS), BF16),
+        pltpu.VMEM((GROUPS, 64, CHUNK), BF16),
+        pltpu.VMEM((CHUNK, COLS), BF16),
+        pltpu.VMEM((CHUNK, COLS), BF16),
         pltpu.VMEM((L, 64, WIDE), F32),
         pltpu.VMEM((16, WIDE + 256), F32),
         pltpu.VMEM((16, WIDE + 256), F32),

time: 27.7 us -> 27.3 us (0.986)
  Pallas kernels: 27 us -> 26.5 us
    pallas_call x1, Pallas kernels: 26.1 us -> 25.7 us  [body(): pl.pallas_call(functools.partial(kernel, n_lon, n_lat), out_shape=(pltpu....]
where the time goes in v5:
time: 27.3 us; the launch traced here: 27.2 us
  Pallas kernels  26.5 us (97%)
  between operations  0.64 us (2%)
    pallas_call x1, Pallas kernels, body(): pl.pallas_call(functools.partial(kernel, n_lon, n_lat), out_shape=(pltpu....  25.7 us
    pallas_call x1, Pallas kernels, body(): pl.pallas_call(finish, out_shape=(tend_shape, field_shape, field_shape),...  0.83 us

profile of v5, /device:TPU:1, one launch (start us, length us, event | category | flops | bytes accessed | tf_op | source)
XLA Modules:
  0.0 27.2 jit_solution(7074227021535706467)
XLA Ops:
  0.6 25.7 %closure_and_sums.1 = (bf16[2,2,8,512]{3,2,1,0:T(8,128)(2,1)S(1)}, f32[24,512]{1,0:T(8,128)S(1)}, f32[1,128]{1,0:T(1,128)S(1)}) custom-call(bf16[48,2,8,512]{3,2,1,0:T(8,128)(2,1)} %feat_hbm.1, bf16[432,480]{1,0:T(8,128)(2,1)} %coef_hbm.1, s32[48,48]{1,0:T(8,128)} %edge_hbm.1, bf16[2,48]{1,0:T(2,128)(2,1)} %head_hbm.1, s32[8,512]{1,0:T(8,128)} %land_hbm.1, ...), custom_call_target="tpu_custom_call" | custom-call | tf_op jit(solution)/shard_map/closure_and_sums/pallas_call | solution.py:470
  26.3 0.8 %finish.1 = (bf16[2,2,8,512]{3,2,1,0:T(8,128)(2,1)}, f32[8,512]{1,0:T(8,128)}, f32[8,512]{1,0:T(8,128)}) custom-call(f32[24,512]{1,0:T(8,128)S(1)} %get-tuple-element.6.fields_ref, f32[1,128]{1,0:T(1,128)S(1)} %get-tuple-element.7.sums_ref, bf16[2,2,8,512]{3,2,1,0:T(8,128)(2,1)S(1)} %get-tuple-element.8.tend_in), custom_call_target="tpu_custom_call" | custom-call | tf_op jit(solution)/shard_map/finish/pallas_call | solution.py:483

commit v6 on v5

--- a/solution.py
+++ b/solution.py
@@ -170,7 +170,7 @@
 
     @pl.when(bottom)
     def _():
-        got[0:3] = jnp.zeros((3, 16, WIDE), F32)
+        got[0:3] = jnp.zeros((3, 16, WIDE), BF16)
 
     for copy in weights_in:
         copy.wait()
@@ -272,11 +272,9 @@
 
     corner = pl.ds(WIDE, 128), pl.ds(WIDE + 128, 128)
     for edge, ref in ((edge_n, north), (edge_s, south)):
-        ref[:, 0:WIDE] = edge
-        ref[:, WIDE : WIDE + 128] = eastern(edge)
-        ref[:, WIDE + 128 :] = western(edge)
-    to_east[...] = eastern(edge_e)
-    to_west[...] = western(edge_e)
+        ref[...] = joined([edge, eastern(edge), western(edge)]).astype(BF16)
+    to_east[...] = eastern(edge_e).astype(BF16)
+    to_west[...] = western(edge_e).astype(BF16)
 
     whole, part = pl.ds(0, WIDE), pl.ds(0, 128)
     upward = jnp.where(top, 3, 0)
@@ -327,8 +325,8 @@
     each(arrivals, lambda copy: copy.wait_recv())
 
     def arrived(k):
-        parts = [got[k, :, 128 * t : 128 * t + 128] for t in range(5)]
-        w, e = got[k + 1, :, 0:128], got[k + 2, :, 0:128]
+        parts = [got[k, :, 128 * t : 128 * t + 128].astype(F32) for t in range(5)]
+        w, e = got[k + 1, :, 0:128].astype(F32), got[k + 2, :, 0:128].astype(F32)
         return [
             parts[0] + jnp.where(low2, w, 0.0), parts[1], parts[2],
             parts[3] + jnp.where(low2, 0.0, e), parts[4] + jnp.where(low2, e, w),
@@ -344,7 +342,7 @@
     flipped = [turned(x) for x in n_parts]
     flipped = flipped[3::-1] + flipped[4:]
     n_rows = joined([jnp.where(top, f, n) for f, n in zip(flipped, n_parts)])
-    from_west, from_east = side[0], side[1]
+    from_west, from_east = side[0].astype(F32), side[1].astype(F32)
 
     def with_sides(x, at):
         count = x.shape[0]
@@ -457,12 +455,12 @@
         pltpu.VMEM((CHUNK, COLS), BF16),
         pltpu.VMEM((CHUNK, COLS), BF16),
         pltpu.VMEM((L, 64, WIDE), F32),
-        pltpu.VMEM((16, WIDE + 256), F32),
-        pltpu.VMEM((16, WIDE + 256), F32),
-        pltpu.VMEM((64, 128), F32),
-        pltpu.VMEM((64, 128), F32),
-        pltpu.VMEM((6, 16, WIDE), F32),
-        pltpu.VMEM((2, 64, 128), F32),
+        pltpu.VMEM((16, WIDE + 256), BF16),
+        pltpu.VMEM((16, WIDE + 256), BF16),
+        pltpu.VMEM((64, 128), BF16),
+        pltpu.VMEM((64, 128), BF16),
+        pltpu.VMEM((6, 16, WIDE), BF16),
+        pltpu.VMEM((2, 64, 128), BF16),
         pltpu.VMEM((n_lat, 1, 128), F32),
         pltpu.VMEM((n_lon, 1, 128), F32),
         dma((GROUPS,)), dma((5,)), dma((8,)), dma((8,)), dma((2,)), dma((2,)),

time: 27.3 us -> 26.2 us (0.960)
  Pallas kernels: 26.5 us -> 25.4 us
    pallas_call x1, Pallas kernels: 25.7 us -> 24.6 us  [body(): pl.pallas_call(functools.partial(kernel, n_lon, n_lat), out_shape=(pltpu....]
where the time goes in v6:
time: 26.2 us; the launch traced here: 26.1 us
  Pallas kernels  25.4 us (97%)
  between operations  0.64 us (2%)
    pallas_call x1, Pallas kernels, body(): pl.pallas_call(functools.partial(kernel, n_lon, n_lat), out_shape=(pltpu....  24.6 us
    pallas_call x1, Pallas kernels, body(): pl.pallas_call(finish, out_shape=(tend_shape, field_shape, field_shape),...  0.83 us

profile of v6, /device:TPU:1, one launch (start us, length us, event | category | flops | bytes accessed | tf_op | source)
XLA Modules:
  0.0 26.1 jit_solution(8503755837773623181)
XLA Ops:
  0.6 24.6 %closure_and_sums.1 = (bf16[2,2,8,512]{3,2,1,0:T(8,128)(2,1)S(1)}, f32[24,512]{1,0:T(8,128)S(1)}, f32[1,128]{1,0:T(1,128)S(1)}) custom-call(bf16[48,2,8,512]{3,2,1,0:T(8,128)(2,1)} %feat_hbm.1, bf16[432,480]{1,0:T(8,128)(2,1)} %coef_hbm.1, s32[48,48]{1,0:T(8,128)} %edge_hbm.1, bf16[2,48]{1,0:T(2,128)(2,1)} %head_hbm.1, s32[8,512]{1,0:T(8,128)} %land_hbm.1, ...), custom_call_target="tpu_custom_call" | custom-call | tf_op jit(solution)/shard_map/closure_and_sums/pallas_call | solution.py:468
  25.2 0.8 %finish.1 = (bf16[2,2,8,512]{3,2,1,0:T(8,128)(2,1)}, f32[8,512]{1,0:T(8,128)}, f32[8,512]{1,0:T(8,128)}) custom-call(f32[24,512]{1,0:T(8,128)S(1)} %get-tuple-element.6.fields_ref, f32[1,128]{1,0:T(1,128)S(1)} %get-tuple-element.7.sums_ref, bf16[2,2,8,512]{3,2,1,0:T(8,128)(2,1)S(1)} %get-tuple-element.8.tend_in), custom_call_target="tpu_custom_call" | custom-call | tf_op jit(solution)/shard_map/finish/pallas_call | solution.py:481

commit v7 on v6

--- a/solution.py
+++ b/solution.py
@@ -37,13 +37,20 @@
     return jnp.where(cond, 1.0, 0.0).astype(BF16)
 
 
-def fold_weights(coef_ref, edge_ref, head_ref, wt, top):
+def selections(spread_ref, offsets_ref, expand_ref):
     channel, lane = iota((C, C * J), 0), iota((C, C * J), 1)
-    spread = ones_where((lane >= channel * J) & (lane < channel * J + J))
-    keep = dot(jnp.where(edge_ref[...] > 0, 1.0, 0.0).astype(BF16), spread).astype(BF16)
+    spread_ref[...] = ones_where((lane >= channel * J) & (lane < channel * J + J))
     o, q = iota((C, 9 * C), 0), iota((C, 9 * C), 1)
-    offset = lax.shift_right_logical(q * 1366, 16)
-    head = dot(head_ref[...], ones_where(q - offset * C == o))
+    offsets_ref[...] = ones_where(q - lax.shift_right_logical(q * 1366, 16) * C == o)
+    q = iota((1, CHUNK), 1)
+    strip = lax.shift_right_logical(q * 13108, 21)
+    source = (2 * strip + (lax.shift_right_logical(q, 3) & 1)) * J + lax.shift_right_logical(q - strip * (2 * ROWS * J), 4)
+    expand_ref[...] = ones_where(iota((GROUP * J, CHUNK), 0) == source)
+
+
+def fold_weights(coef_ref, edge_ref, head_ref, spread_ref, offsets_ref):
+    keep = dot(jnp.where(edge_ref[...] > 0, 1.0, 0.0).astype(BF16), spread_ref[...]).astype(BF16)
+    head = dot(head_ref[...], offsets_ref[...])
     r, q = iota((24, 9 * C), 0), iota((24, 9 * C), 1)
     offset = lax.shift_right_logical(q * 1366, 16)
     head = jnp.where((r & 1) == 0, head[0:1], head[1:2])
@@ -55,16 +62,16 @@
     off = jnp.abs(j - NB // 2).astype(F32)
     scale = jnp.where(j == NB, 2.0**LIFT, jnp.exp(-off * off))
     folded = folded * scale
-    q = iota((1, CHUNK), 1)
-    strip = lax.shift_right_logical(q * 13108, 21)
-    source = (2 * strip + (lax.shift_right_logical(q, 3) & 1)) * J + lax.shift_right_logical(q - strip * (2 * ROWS * J), 4)
-    expand = ones_where(iota((GROUP * J, CHUNK), 0) == source)
+    return folded
+
+
+def band_weights(folded, expand_ref, wt, top):
     y_out = iota((ROWS, CHUNK), 0)
     y_in = iota((ROWS, CHUNK), 1) & 7
     first_row, last_row = y_in[0:6] == 0, y_in[0:6] == 7
     pad = jnp.zeros((2, CHUNK), F32)
     for group in range(GROUPS):
-        g = dot(folded[:, GROUP * J * group : GROUP * J * (group + 1)].astype(BF16), expand)
+        g = dot(folded[:, GROUP * J * group : GROUP * J * (group + 1)].astype(BF16), expand_ref[...])
         tiles = []
         for k in range(6):
             tile = jnp.where(y_in == y_out - 1, g[k : k + 1], 0.0)
@@ -97,8 +104,8 @@
     n_lon, n_lat,
     feat_hbm, coef_hbm, edge_hbm, head_hbm, land_hbm, shift_hbm,
     tend_ref, fields_ref, sums_ref,
-    feat, coef_ref, edge_ref, head_ref, land_ref, shift_ref, wt, bases_a, bases_b, acc,
-    north, south, to_east, to_west, got, side, sums_a, sums_b,
+    feat, coef_ref, edge_ref, head_ref, land_ref, shift_ref, spread_ref, offsets_ref, expand_ref, wt, bases_a, bases_b, acc,
+    north, south, to_east, to_west, got, side, sums_a, sums_b, sums_d,
     feat_sem, weight_sem, send, recv, send_sum, recv_sum,
 ):
     lon, lat = lax.axis_index("lon"), lax.axis_index("lat")
@@ -140,6 +147,14 @@
     second_order = far_first(n_lon, lambda d: (0, 1, 2, 1)[d % 4] + (0, 2, 1, 1)[d // 4 % 4])
     second_sum = [(bits(lon, 2 * (d % half)), bits(lat, d // half)) for d in second_order]
     second_here = lon // 2 + half * lax.rem(lat, 2)
+    hubs = [(a, b) for b in (0, 2) for a in range(4)]
+
+    def is_hub(at_lon, at_lat):
+        return (at_lon < 4) & ((at_lat == 0) | (at_lat == 2))
+
+    hub, hub_plane = is_hub(lon, lat), lat < 4
+    direct_here = lon * n_lat + lat
+
 
     barrier = pltpu.get_barrier_semaphore()
 
@@ -160,7 +175,20 @@
 
     for at in first_sum + second_sum:
         greet(*at)
-    greetings = n_lon + n_lat + 6 - jnp.where(east_self, 1, 0) - jnp.where(west_self, 1, 0) - jnp.where(bottom, 3, 0)
+
+    @pl.when(hub)
+    def _():
+        for f in range(1, n_lon):
+            greet(bits(lon, f), lat)
+
+        def band(b, carry):
+            for f in range(n_lon):
+                greet(bits(lon, f), jnp.bitwise_xor(lat, b))
+            return carry
+
+        lax.fori_loop(1, n_lat, band, 0)
+
+    greetings = n_lon + n_lat + 6 - jnp.where(east_self, 1, 0) - jnp.where(west_self, 1, 0) - jnp.where(bottom, 3, 0) + len(hubs) - jnp.where(hub, 1, 0)
 
     def remote(src, dst, send, recv, at_lon, at_lat):
         return pltpu.make_async_remote_copy(
@@ -172,12 +200,16 @@
     def _():
         got[0:3] = jnp.zeros((3, 16, WIDE), BF16)
 
-    for copy in weights_in:
+    selections(spread_ref, offsets_ref, expand_ref)
+    acc[...] = jnp.zeros(acc.shape, F32)
+    for copy in weights_in[:3]:
+        copy.wait()
+    folded = fold_weights(coef_ref, edge_ref, head_ref, spread_ref, offsets_ref)
+    for copy in weights_in[3:]:
         copy.wait()
     feat_in(0).wait()
-    fold_weights(coef_ref, edge_ref, head_ref, wt, top)
-
-    acc[...] = jnp.zeros(acc.shape, F32)
+    band_weights(folded, expand_ref, wt, top)
+
 
     def expanded(k, out):
         for at in range(0, GROUP, 2):
@@ -390,40 +422,58 @@
 
     dots = [summed(r * r), summed(r * q1), summed(q1 * q1), summed(r * q2), summed(q1 * q2)]
 
-    def spread(value, ref, stage, here, devices):
-        ref[here] = value
-        copies = [remote(ref.at[here], ref.at[here], send_sum.at[stage], recv_sum.at[stage], *at) for at in devices]
-        for copy in copies:
-            copy.start()
-
-    def all_copies(ref, stage, count):
-        several = ref.at[pl.ds(0, count - 1)]
+    def row_to(ref, stage, here, at):
+        remote(ref.at[here], ref.at[here], send_sum.at[stage], recv_sum.at[stage], *at).start()
+
+    def rows_of(ref, stage, number):
+        several = ref.at[pl.ds(0, number)]
         return remote(several, several, send_sum.at[stage], recv_sum.at[stage], east, lat)
-
-    def collect(ref, stage, count):
-        all_copies(ref, stage, count).wait_recv()
-        return jnp.sum(ref[...], axis=0)
 
     dots = jnp.sum(stacked(dots + [jnp.zeros((3, 128), F32)]), axis=1, keepdims=True)
     dots = jnp.sum(jnp.where(lane == iota((ROWS, 128), 0), dots, 0.0), axis=0, keepdims=True)
-    spread(dots, sums_a, 0, first_here, first_sum)
-
-    ocean = ocean[:, 0:COLS]
-    upper = with_sides(upper, 32)
-    for c in range(2):
-        one_level = upper[8 * c : 8 * c + 8] + placed([(0, one(s_rows, 8 + c)), (7, one(n_rows, 8 + c))])
-        one_level = ocean * one_level[:, 0:COLS]
-        whole = (eastward, northward)[c][0:8, 0:COLS]
-        tend_ref[c, 0] = (whole - one_level).astype(BF16)
-        tend_ref[c, 1] = one_level.astype(BF16)
-    for k, value in enumerate((r, q1, q2)):
-        fields_ref[8 * k : 8 * k + 8, :] = value
+    sums_d[direct_here] = dots
+    sums_a[first_here] = dots
+    for at in hubs:
+        other = (lon != at[0]) | (lat != at[1])
+        pl.when(other)(functools.partial(row_to, sums_d, 2, direct_here, at))
+    for at in first_sum:
+        row_to(sums_a, 0, first_here, at)
+
+    @pl.when(lat >= 0)
+    def _():
+        second = with_sides(upper, 32)
+        for c in range(2):
+            one_level = second[8 * c : 8 * c + 8] + placed([(0, one(s_rows, 8 + c)), (7, one(n_rows, 8 + c))])
+            one_level = ocean[:, 0:COLS] * one_level[:, 0:COLS]
+            whole = (eastward, northward)[c][0:8, 0:COLS]
+            tend_ref[c, 0] = (whole - one_level).astype(BF16)
+            tend_ref[c, 1] = one_level.astype(BF16)
+        for k, value in enumerate((r, q1, q2)):
+            fields_ref[8 * k : 8 * k + 8, :] = value
+
     each(sends, lambda copy: copy.wait_send())
 
-    spread(collect(sums_a, 0, n_lat), sums_b, 1, second_here, second_sum)
-    sums_ref[...] = collect(sums_b, 1, n_lon)
-    all_copies(sums_a, 0, n_lat).wait_send()
-    all_copies(sums_b, 1, n_lon).wait_send()
+    rows_of(sums_a, 0, n_lat - 1).wait_recv()
+    sums_b[second_here] = jnp.sum(sums_a[...], axis=0)
+    for at in second_sum:
+        pl.when(jnp.logical_not(is_hub(*at)))(functools.partial(row_to, sums_b, 1, second_here, at))
+
+    @pl.when(hub)
+    def _():
+        rows_of(sums_d, 2, n_lon * n_lat - 1).wait_recv()
+        sums_ref[...] = jnp.sum(sums_d[...], axis=0)
+        rows_of(sums_d, 2, len(hubs) - 1).wait_send()
+        rows_of(sums_b, 1, n_lon - 2).wait_send()
+
+    @pl.when(jnp.logical_not(hub))
+    def _():
+        rows_of(sums_b, 1, n_lon - 1).wait_recv()
+        sums_ref[...] = jnp.sum(sums_b[...], axis=0)
+        rows_of(sums_d, 2, len(hubs)).wait_send()
+        pl.when(hub_plane)(lambda: rows_of(sums_b, 1, n_lon - 3).wait_send())
+        pl.when(jnp.logical_not(hub_plane))(lambda: rows_of(sums_b, 1, n_lon - 1).wait_send())
+
+    rows_of(sums_a, 0, n_lat - 1).wait_send()
 
 
 def finish(fields_ref, sums_ref, tend_in, tend_ref, surf_ref, res_ref):
@@ -451,6 +501,9 @@
         pltpu.VMEM((2, C), BF16),
         pltpu.VMEM((ROWS, COLS), jnp.int32),
         pltpu.VMEM((ROWS, COLS), F32),
+        pltpu.VMEM((C, C * J), BF16),
+        pltpu.VMEM((C, 9 * C), BF16),
+        pltpu.VMEM((GROUP * J, CHUNK), BF16),
         pltpu.VMEM((GROUPS, 64, CHUNK), BF16),
         pltpu.VMEM((CHUNK, COLS), BF16),
         pltpu.VMEM((CHUNK, COLS), BF16),
@@ -463,7 +516,8 @@
         pltpu.VMEM((2, 64, 128), BF16),
         pltpu.VMEM((n_lat, 1, 128), F32),
         pltpu.VMEM((n_lon, 1, 128), F32),
-        dma((GROUPS,)), dma((5,)), dma((8,)), dma((8,)), dma((2,)), dma((2,)),
+        pltpu.VMEM((n_lon * n_lat, 1, 128), F32),
+        dma((GROUPS,)), dma((5,)), dma((8,)), dma((8,)), dma((3,)), dma((3,)),
     ]
     tendency, fields, sums = pl.pallas_call(
         functools.partial(kernel, n_lon, n_lat),

time: 26.2 us -> 25.1 us (0.958)
  Pallas kernels: 25.4 us -> 24.3 us
    pallas_call x1, Pallas kernels: 24.6 us -> 23.5 us  [body(): pl.pallas_call(functools.partial(kernel, n_lon, n_lat), out_shape=(pltpu....]
where the time goes in v7:
time: 25.1 us; the launch traced here: 24.9 us
  Pallas kernels  24.3 us (97%)
  between operations  0.64 us (3%)
    pallas_call x1, Pallas kernels, body(): pl.pallas_call(functools.partial(kernel, n_lon, n_lat), out_shape=(pltpu....  23.5 us
    pallas_call x1, Pallas kernels, body(): pl.pallas_call(finish, out_shape=(tend_shape, field_shape, field_shape),...  0.83 us

profile of v7, /device:TPU:1, one launch (start us, length us, event | category | flops | bytes accessed | tf_op | source)
XLA Modules:
  0.0 24.9 jit_solution(11765815414429929106)
XLA Ops:
  0.6 23.5 %closure_and_sums.1 = (bf16[2,2,8,512]{3,2,1,0:T(8,128)(2,1)S(1)}, f32[24,512]{1,0:T(8,128)S(1)}, f32[1,128]{1,0:T(1,128)S(1)}) custom-call(bf16[48,2,8,512]{3,2,1,0:T(8,128)(2,1)} %feat_hbm.1, bf16[432,480]{1,0:T(8,128)(2,1)} %coef_hbm.1, s32[48,48]{1,0:T(8,128)} %edge_hbm.1, bf16[2,48]{1,0:T(2,128)(2,1)} %head_hbm.1, s32[8,512]{1,0:T(8,128)} %land_hbm.1, ...), custom_call_target="tpu_custom_call" | custom-call | tf_op jit(solution)/shard_map/closure_and_sums/pallas_call | solution.py:522
  24.1 0.8 %finish.1 = (bf16[2,2,8,512]{3,2,1,0:T(8,128)(2,1)}, f32[8,512]{1,0:T(8,128)}, f32[8,512]{1,0:T(8,128)}) custom-call(f32[24,512]{1,0:T(8,128)S(1)} %get-tuple-element.6.fields_ref, f32[1,128]{1,0:T(1,128)S(1)} %get-tuple-element.7.sums_ref, bf16[2,2,8,512]{3,2,1,0:T(8,128)(2,1)S(1)} %get-tuple-element.8.tend_in), custom_call_target="tpu_custom_call" | custom-call | tf_op jit(solution)/shard_map/finish/pallas_call | solution.py:535

commit v8 on v7

--- a/solution.py
+++ b/solution.py
@@ -108,6 +108,20 @@
     north, south, to_east, to_west, got, side, sums_a, sums_b, sums_d,
     feat_sem, weight_sem, send, recv, send_sum, recv_sum,
 ):
+    weights_in = [
+        pltpu.make_async_copy(src, dst, weight_sem.at[k])
+        for k, (src, dst) in enumerate(
+            [(edge_hbm, edge_ref), (head_hbm, head_ref), (coef_hbm, coef_ref), (land_hbm, land_ref), (shift_hbm, shift_ref)]
+        )
+    ]
+
+    def feat_in(k):
+        part = pl.ds(k * GROUP, GROUP)
+        return pltpu.make_async_copy(feat_hbm.at[part], feat.at[part], feat_sem.at[k])
+
+    for copy in weights_in + [feat_in(k) for k in range(GROUPS)]:
+        copy.start()
+
     lon, lat = lax.axis_index("lon"), lax.axis_index("lat")
     top, bottom = lat == n_lat - 1, lat == 0
     east = jnp.where(lon == n_lon - 1, 0, lon + 1)
@@ -121,20 +135,6 @@
     east_other, west_other = jnp.logical_not(east_self), jnp.logical_not(west_self)
     has_south = jnp.logical_not(bottom)
 
-    weights_in = [
-        pltpu.make_async_copy(src, dst, weight_sem.at[k])
-        for k, (src, dst) in enumerate(
-            [(edge_hbm, edge_ref), (head_hbm, head_ref), (coef_hbm, coef_ref), (land_hbm, land_ref), (shift_hbm, shift_ref)]
-        )
-    ]
-
-    def feat_in(k):
-        part = pl.ds(k * GROUP, GROUP)
-        return pltpu.make_async_copy(feat_hbm.at[part], feat.at[part], feat_sem.at[k])
-
-    for copy in weights_in + [feat_in(k) for k in range(GROUPS)]:
-        copy.start()
-
     half = n_lon // 2
     ring = {0: 0, 1: 1, 2: 2, 3: 3, 4: 4, 5: 3, 6: 2, 7: 2}
 
@@ -147,12 +147,13 @@
     second_order = far_first(n_lon, lambda d: (0, 1, 2, 1)[d % 4] + (0, 2, 1, 1)[d // 4 % 4])
     second_sum = [(bits(lon, 2 * (d % half)), bits(lat, d // half)) for d in second_order]
     second_here = lon // 2 + half * lax.rem(lat, 2)
-    hubs = [(a, b) for b in (0, 2) for a in range(4)]
+    hub_lon, hub_lat = max(2, n_lon // 4), max(2, n_lat // 4)
+    hubs = [(a, b) for b in range(hub_lat) for a in range(hub_lon)]
 
     def is_hub(at_lon, at_lat):
-        return (at_lon < 4) & ((at_lat == 0) | (at_lat == 2))
-
-    hub, hub_plane = is_hub(lon, lat), lat < 4
+        return (at_lon < hub_lon) & (at_lat < hub_lat)
+
+    hub, hub_plane = is_hub(lon, lat), lat < hub_lat
     direct_here = lon * n_lat + lat
 
 
@@ -431,11 +432,12 @@
 
     dots = jnp.sum(stacked(dots + [jnp.zeros((3, 128), F32)]), axis=1, keepdims=True)
     dots = jnp.sum(jnp.where(lane == iota((ROWS, 128), 0), dots, 0.0), axis=0, keepdims=True)
-    sums_d[direct_here] = dots
+    direct_row = sums_d.at[pl.ds(direct_here, 1)]
+    direct_row[...] = dots
     sums_a[first_here] = dots
     for at in hubs:
         other = (lon != at[0]) | (lat != at[1])
-        pl.when(other)(functools.partial(row_to, sums_d, 2, direct_here, at))
+        pl.when(other)(remote(direct_row, direct_row, send_sum.at[2], recv_sum.at[2], *at).start)
     for at in first_sum:
         row_to(sums_a, 0, first_here, at)
 
@@ -461,16 +463,16 @@
     @pl.when(hub)
     def _():
         rows_of(sums_d, 2, n_lon * n_lat - 1).wait_recv()
-        sums_ref[...] = jnp.sum(sums_d[...], axis=0)
+        sums_ref[...] = jnp.sum(sums_d[...], axis=0, keepdims=True)
         rows_of(sums_d, 2, len(hubs) - 1).wait_send()
-        rows_of(sums_b, 1, n_lon - 2).wait_send()
+        rows_of(sums_b, 1, n_lon - hub_lon).wait_send()
 
     @pl.when(jnp.logical_not(hub))
     def _():
         rows_of(sums_b, 1, n_lon - 1).wait_recv()
         sums_ref[...] = jnp.sum(sums_b[...], axis=0)
         rows_of(sums_d, 2, len(hubs)).wait_send()
-        pl.when(hub_plane)(lambda: rows_of(sums_b, 1, n_lon - 3).wait_send())
+        pl.when(hub_plane)(lambda: rows_of(sums_b, 1, n_lon - 1 - hub_lon).wait_send())
         pl.when(jnp.logical_not(hub_plane))(lambda: rows_of(sums_b, 1, n_lon - 1).wait_send())
 
     rows_of(sums_a, 0, n_lat - 1).wait_send()
@@ -516,7 +518,7 @@
         pltpu.VMEM((2, 64, 128), BF16),
         pltpu.VMEM((n_lat, 1, 128), F32),
         pltpu.VMEM((n_lon, 1, 128), F32),
-        pltpu.VMEM((n_lon * n_lat, 1, 128), F32),
+        pltpu.VMEM((n_lon * n_lat, 128), F32),
         dma((GROUPS,)), dma((5,)), dma((8,)), dma((8,)), dma((3,)), dma((3,)),
     ]
     tendency, fields, sums = pl.pallas_call(

time: 25.1 us -> 24.8 us (0.988)
  no operation moved by 1% of the time
where the time goes in v8:
time: 24.8 us; the launch traced here: 24.7 us
  Pallas kernels  24.1 us (97%)
  between operations  0.64 us (3%)
    pallas_call x1, Pallas kernels, body(): pl.pallas_call(functools.partial(kernel, n_lon, n_lat), out_shape=(pltpu....  23.3 us
    pallas_call x1, Pallas kernels, body(): pl.pallas_call(finish, out_shape=(tend_shape, field_shape, field_shape),...  0.83 us

profile of v8, /device:TPU:1, one launch (start us, length us, event | category | flops | bytes accessed | tf_op | source)
XLA Modules:
  0.0 24.7 jit_solution(11931932474104821967)
XLA Ops:
  0.6 23.3 %closure_and_sums.1 = (bf16[2,2,8,512]{3,2,1,0:T(8,128)(2,1)S(1)}, f32[24,512]{1,0:T(8,128)S(1)}, f32[1,128]{1,0:T(1,128)S(1)}) custom-call(bf16[48,2,8,512]{3,2,1,0:T(8,128)(2,1)} %feat_hbm.1, bf16[432,480]{1,0:T(8,128)(2,1)} %coef_hbm.1, s32[48,48]{1,0:T(8,128)} %edge_hbm.1, bf16[2,48]{1,0:T(2,128)(2,1)} %head_hbm.1, s32[8,512]{1,0:T(8,128)} %land_hbm.1, ...), custom_call_target="tpu_custom_call" | custom-call | tf_op jit(solution)/shard_map/closure_and_sums/pallas_call | solution.py:524
  23.9 0.8 %finish.1 = (bf16[2,2,8,512]{3,2,1,0:T(8,128)(2,1)}, f32[8,512]{1,0:T(8,128)}, f32[8,512]{1,0:T(8,128)}) custom-call(f32[24,512]{1,0:T(8,128)S(1)} %get-tuple-element.6.fields_ref, f32[1,128]{1,0:T(1,128)S(1)} %get-tuple-element.7.sums_ref, bf16[2,2,8,512]{3,2,1,0:T(8,128)(2,1)S(1)} %get-tuple-element.8.tend_in), custom_call_target="tpu_custom_call" | custom-call | tf_op jit(solution)/shard_map/finish/pallas_call | solution.py:537

commit v9 on v8

--- a/solution.py
+++ b/solution.py
@@ -147,13 +147,16 @@
     second_order = far_first(n_lon, lambda d: (0, 1, 2, 1)[d % 4] + (0, 2, 1, 1)[d // 4 % 4])
     second_sum = [(bits(lon, 2 * (d % half)), bits(lat, d // half)) for d in second_order]
     second_here = lon // 2 + half * lax.rem(lat, 2)
-    hub_lon, hub_lat = max(2, n_lon // 4), max(2, n_lat // 4)
-    hubs = [(a, b) for b in range(hub_lat) for a in range(hub_lon)]
+    hubs = [(1, 0), (0, 2), (2, 0), (0, 1), (1, 2), (2, 2), (0, 4), (4, 0), (6, 0)]
 
     def is_hub(at_lon, at_lat):
-        return (at_lon < hub_lon) & (at_lat < hub_lat)
-
-    hub, hub_plane = is_hub(lon, lat), lat < hub_lat
+        return functools.reduce(jnp.logical_or, [(at_lon == a) & (at_lat == b) for a, b in hubs])
+
+    hub = is_hub(lon, lat)
+    beside = sum(
+        jnp.where((lat // 2 == b // 2) & (lax.rem(lon, 2) == a % 2) & ((lon != a) | (lat != b)), 1, 0) for a, b in hubs
+    )
+    most = max(sum(1 for a, b in hubs if b // 2 == z and a % 2 == c) for z in range(n_lat // 2) for c in range(2))
     direct_here = lon * n_lat + lat
 
 
@@ -184,7 +187,7 @@
 
         def band(b, carry):
             for f in range(n_lon):
-                greet(bits(lon, f), jnp.bitwise_xor(lat, b))
+                greet(bits(lon, f), jnp.bitwise_xor(lat, n_lat - b))
             return carry
 
         lax.fori_loop(1, n_lat, band, 0)
@@ -465,16 +468,15 @@
         rows_of(sums_d, 2, n_lon * n_lat - 1).wait_recv()
         sums_ref[...] = jnp.sum(sums_d[...], axis=0, keepdims=True)
         rows_of(sums_d, 2, len(hubs) - 1).wait_send()
-        rows_of(sums_b, 1, n_lon - hub_lon).wait_send()
 
     @pl.when(jnp.logical_not(hub))
     def _():
         rows_of(sums_b, 1, n_lon - 1).wait_recv()
         sums_ref[...] = jnp.sum(sums_b[...], axis=0)
         rows_of(sums_d, 2, len(hubs)).wait_send()
-        pl.when(hub_plane)(lambda: rows_of(sums_b, 1, n_lon - 1 - hub_lon).wait_send())
-        pl.when(jnp.logical_not(hub_plane))(lambda: rows_of(sums_b, 1, n_lon - 1).wait_send())
-
+
+    for k in range(most + 1):
+        pl.when(beside == k)(rows_of(sums_b, 1, n_lon - 1 - k).wait_send)
     rows_of(sums_a, 0, n_lat - 1).wait_send()
 
 

time: 24.8 us -> 24.8 us (level)
  no operation moved by 1% of the time
where the time goes in v9:
time: 24.8 us; the launch traced here: 24.7 us
  Pallas kernels  24.1 us (97%)
  between operations  0.64 us (3%)
    pallas_call x1, Pallas kernels, body(): pl.pallas_call(functools.partial(kernel, n_lon, n_lat), out_shape=(pltpu....  23.2 us
    pallas_call x1, Pallas kernels, body(): pl.pallas_call(finish, out_shape=(tend_shape, field_shape, field_shape),...  0.83 us

profile of v9, /device:TPU:1, one launch (start us, length us, event | category | flops | bytes accessed | tf_op | source)
XLA Modules:
  0.0 24.7 jit_solution(11842862338553220417)
XLA Ops:
  0.6 23.2 %closure_and_sums.1 = (bf16[2,2,8,512]{3,2,1,0:T(8,128)(2,1)S(1)}, f32[24,512]{1,0:T(8,128)S(1)}, f32[1,128]{1,0:T(1,128)S(1)}) custom-call(bf16[48,2,8,512]{3,2,1,0:T(8,128)(2,1)} %feat_hbm.1, bf16[432,480]{1,0:T(8,128)(2,1)} %coef_hbm.1, s32[48,48]{1,0:T(8,128)} %edge_hbm.1, bf16[2,48]{1,0:T(2,128)(2,1)} %head_hbm.1, s32[8,512]{1,0:T(8,128)} %land_hbm.1, ...), custom_call_target="tpu_custom_call" | custom-call | tf_op jit(solution)/shard_map/closure_and_sums/pallas_call | solution.py:526
  23.9 0.8 %finish.1 = (bf16[2,2,8,512]{3,2,1,0:T(8,128)(2,1)}, f32[8,512]{1,0:T(8,128)}, f32[8,512]{1,0:T(8,128)}) custom-call(f32[24,512]{1,0:T(8,128)S(1)} %get-tuple-element.6.fields_ref, f32[1,128]{1,0:T(1,128)S(1)} %get-tuple-element.7.sums_ref, bf16[2,2,8,512]{3,2,1,0:T(8,128)(2,1)S(1)} %get-tuple-element.8.tend_in), custom_call_target="tpu_custom_call" | custom-call | tf_op jit(solution)/shard_map/finish/pallas_call | solution.py:539

commit v10 on v8

--- a/solution.py
+++ b/solution.py
@@ -247,6 +247,8 @@
             for c in range(2):
                 acc[level, 16 + 8 * c : 17 + 8 * c, 0:COLS] += outside[c : c + 1] + outside[c + 2 : c + 3] + outside[c + 4 : c + 5]
 
+    pl.semaphore_wait(barrier, greetings)
+
     lane, low = iota((ROWS, 128), 1), iota((ROWS, 128), 1) < 64
     low2 = iota((16, 128), 1) < 64
     row = iota((ROWS, WIDE), 0)
@@ -295,7 +297,6 @@
     edge_s = stacked(
         [total_down] + both(0) + both(1) + none * 2 + [below[1], ocean[0:1], ocean[1:2]] + none + [shift[0:1]] + none * 2
     )
-    edge_e = stacked(share + [upper, ocean, shift])
 
     def eastern(x):
         return jnp.where(iota((x.shape[0], 128), 1) < 64, x[:, COLS:], x[:, COLS - 128 : COLS])
@@ -306,8 +307,6 @@
     corner = pl.ds(WIDE, 128), pl.ds(WIDE + 128, 128)
     for edge, ref in ((edge_n, north), (edge_s, south)):
         ref[...] = joined([edge, eastern(edge), western(edge)]).astype(BF16)
-    to_east[...] = eastern(edge_e).astype(BF16)
-    to_west[...] = western(edge_e).astype(BF16)
 
     whole, part = pl.ds(0, WIDE), pl.ds(0, 128)
     upward = jnp.where(top, 3, 0)
@@ -344,8 +343,11 @@
             else:
                 pl.when(cond)(functools.partial(act, copy))
 
-    pl.semaphore_wait(barrier, greetings)
-    each(sends, lambda copy: copy.start())
+    each(sends[:6], lambda copy: copy.start())
+    edge_e = stacked(share + [upper, ocean, shift])
+    to_east[...] = eastern(edge_e).astype(BF16)
+    to_west[...] = western(edge_e).astype(BF16)
+    each(sends[6:], lambda copy: copy.start())
 
     @pl.when(east_self)
     def _():
@@ -417,11 +419,11 @@
     q2 = operate(q1)[0:8, 0:COLS]
     r, q1 = r[0:8, 0:COLS], q1[0:8, 0:COLS]
 
-    def summed(x):
+    dots = zero[:, 0:128]
+    for k, x in enumerate((r * r, r * q1, q1 * q1, r * q2, q1 * q2)):
         x = x[:, 0:128] + x[:, 128:256] + x[:, 256:384] + x[:, 384:512]
-        return jnp.sum(x, axis=0, keepdims=True)
-
-    dots = [summed(r * r), summed(r * q1), summed(q1 * q1), summed(r * q2), summed(q1 * q2)]
+        dots = jnp.where(lane == k, jnp.sum(x, axis=1, keepdims=True), dots)
+    dots = jnp.sum(dots, axis=0, keepdims=True)
 
     def row_to(ref, stage, here, at):
         remote(ref.at[here], ref.at[here], send_sum.at[stage], recv_sum.at[stage], *at).start()
@@ -430,8 +432,6 @@
         several = ref.at[pl.ds(0, number)]
         return remote(several, several, send_sum.at[stage], recv_sum.at[stage], east, lat)
 
-    dots = jnp.sum(stacked(dots + [jnp.zeros((3, 128), F32)]), axis=1, keepdims=True)
-    dots = jnp.sum(jnp.where(lane == iota((ROWS, 128), 0), dots, 0.0), axis=0, keepdims=True)
     direct_row = sums_d.at[pl.ds(direct_here, 1)]
     direct_row[...] = dots
     sums_a[first_here] = dots

time: 24.8 us -> 24.8 us (level)
  no operation moved by 1% of the time
where the time goes in v10:
time: 24.8 us; the launch traced here: 24.7 us
  Pallas kernels  24.1 us (97%)
  between operations  0.64 us (3%)
    pallas_call x1, Pallas kernels, body(): pl.pallas_call(functools.partial(kernel, n_lon, n_lat), out_shape=(pltpu....  23.3 us
    pallas_call x1, Pallas kernels, body(): pl.pallas_call(finish, out_shape=(tend_shape, field_shape, field_shape),...  0.83 us

profile of v10, /device:TPU:1, one launch (start us, length us, event | category | flops | bytes accessed | tf_op | source)
XLA Modules:
  0.0 24.7 jit_solution(16922914580738416679)
XLA Ops:
  0.6 23.3 %closure_and_sums.1 = (bf16[2,2,8,512]{3,2,1,0:T(8,128)(2,1)S(1)}, f32[24,512]{1,0:T(8,128)S(1)}, f32[1,128]{1,0:T(1,128)S(1)}) custom-call(bf16[48,2,8,512]{3,2,1,0:T(8,128)(2,1)} %feat_hbm.1, bf16[432,480]{1,0:T(8,128)(2,1)} %coef_hbm.1, s32[48,48]{1,0:T(8,128)} %edge_hbm.1, bf16[2,48]{1,0:T(2,128)(2,1)} %head_hbm.1, s32[8,512]{1,0:T(8,128)} %land_hbm.1, ...), custom_call_target="tpu_custom_call" | custom-call | tf_op jit(solution)/shard_map/closure_and_sums/pallas_call | solution.py:524
  23.9 0.8 %finish.1 = (bf16[2,2,8,512]{3,2,1,0:T(8,128)(2,1)}, f32[8,512]{1,0:T(8,128)}, f32[8,512]{1,0:T(8,128)}) custom-call(f32[24,512]{1,0:T(8,128)S(1)} %get-tuple-element.6.fields_ref, f32[1,128]{1,0:T(1,128)S(1)} %get-tuple-element.7.sums_ref, bf16[2,2,8,512]{3,2,1,0:T(8,128)(2,1)S(1)} %get-tuple-element.8.tend_in), custom_call_target="tpu_custom_call" | custom-call | tf_op jit(solution)/shard_map/finish/pallas_call | solution.py:537
